TPU v7x, 32 devices: a whole 2x2x4 slice. The times are simulated.
32 devices in a mesh: dp: 4 (over z), fsdp: 8 (over y, x, core).
Axes of the slice: x: 2, y: 2, z: 4, core: 2. Of those that a mesh axis runs over, the one named last changes fastest.
Arguments:
- tokens: bfloat16 [32768, 768], P(('dp', 'fsdp')), may hold values from -6 to 6
- first_values: bfloat16 [32768, 384], P(('dp', 'fsdp')), may hold values from -6 to 6
- cotangent: bfloat16 [32768, 768], P(('dp', 'fsdp')), may hold values from -6 to 6
- lengths: int32 [32, 2], P(('dp', 'fsdp')), may hold values from 0 to 1024, as said below
- vectors: float32 [8832], P('fsdp'), may hold values from -1 to 1.5
- w_qkv: bfloat16 [768, 1920], P(('dp', 'fsdp')), may hold values from -0.21875 to 0.21875
- w_out: bfloat16 [768, 768], P(('dp', 'fsdp')), may hold values from -1.75 to 1.75
- w_up: bfloat16 [768, 3072], P(('dp', 'fsdp')), may hold values from -0.21875 to 0.21875
- w_down: bfloat16 [3072, 768], P(('dp', 'fsdp')), may hold values from -0.109375 to 0.109375
Outputs:
- output: bfloat16 [32768, 768], P(('dp', 'fsdp'))
- grad_tokens: bfloat16 [32768, 768], P(('dp', 'fsdp'))
- grad_first_values: bfloat16 [32768, 384], P(('dp', 'fsdp'))
- grad_vectors: float32 [8832], P('fsdp')
- grad_qkv: float32 [768, 1920], P(('dp', 'fsdp'))
- grad_out: float32 [768, 768], P(('dp', 'fsdp'))
- grad_up: float32 [768, 3072], P(('dp', 'fsdp'))
- grad_down: float32 [3072, 768], P(('dp', 'fsdp'))
Inputs may be any that keep to these rules, and one draw needn't show every extreme that they name: `lengths`: each row is either (1024, 0) or (512, 512); the first row is the former and the last row the latter.
All inputs are finite; a program needn't handle non-finite values.
Results may differ from a plain program's by a relative error of at most 0.012.
Values may be sent and summed in bfloat16 or wider, within the bound.
No kernel may reach another device: no remote copies, remote signals or barrier semaphores. Data moves between devices by JAX's collectives and lax.ppermute only.
A program may use at most 320 MiB of HBM per device.

v0:
```python
import functools
import math

import jax
import jax.numpy as jnp
from jax import lax
from jax.experimental import pallas as pl
from jax.experimental.pallas import tpu as pltpu
from jax.sharding import PartitionSpec as P

BF = jnp.bfloat16
F32 = jnp.float32
HD = 64
EPSILON = 1e-5
HIDDEN = -1e30
AXES = ("dp", "fsdp")
GELU = math.sqrt(2 / math.pi)
CUBE = 0.044715
MIB = 1 << 20
VMEM = 60
PACE = 0.01


def nn(a, b):
    return jnp.dot(a, b, preferred_element_type=F32)


def nt(a, b):
    return lax.dot_general(a, b, (((1,), (1,)), ((), ())), preferred_element_type=F32)


def tn(a, b):
    return lax.dot_general(a, b, (((0,), (0,)), ((), ())), preferred_element_type=F32)


def shape_of(shape, dtype=BF):
    return jax.ShapeDtypeStruct(shape, dtype)


def whole(a):
    return pl.BlockSpec(a.shape, lambda i: (0,) * a.ndim, pipeline_mode=pl.Buffered(1))


def kept(a):
    return pl.BlockSpec(a.shape, lambda *at: (0,) * a.ndim, pipeline_mode=pl.Buffered(1))


def rows_of(blk, n):
    return pl.BlockSpec((blk, n), lambda i: (i, 0))


def vector_of(n):
    return pl.BlockSpec((1, n), lambda i: (0, 0))


SCALARS = pl.BlockSpec(memory_space=pltpu.SMEM)


class Chain:
    def __init__(self):
        self.mark = None

    def call(
        self, kernel, args, *, grid, in_specs, out_specs, out_shape, vmem, cost, waits=(), into=None, scalars=0,
        scratch_shapes=(), name=None,
    ):
        several = isinstance(out_shape, (list, tuple))
        out_specs = list(out_specs) if several else [out_specs]
        out_shape = list(out_shape) if several else [out_shape]
        into = list(into or ())
        deps = into + ([] if self.mark is None else [self.mark]) + list(waits)
        used, extra, outs = len(args), len(deps), len(out_shape)

        def body(*refs):
            results = used + extra
            mark = refs[results + outs]
            mark[...] = jnp.zeros(mark.shape, mark.dtype)
            kernel(*refs[:used], *refs[results : results + outs], *refs[results + outs + 1 :])

        got = pl.pallas_call(
            body,
            grid_spec=pltpu.PrefetchScalarGridSpec(
                num_scalar_prefetch=scalars,
                grid=grid,
                in_specs=list(in_specs) + [pl.BlockSpec(memory_space=pl.ANY)] * extra,
                out_specs=out_specs + [pl.BlockSpec((8, 128), lambda *at: (0, 0))],
                scratch_shapes=list(scratch_shapes),
            ),
            out_shape=out_shape + [shape_of((8, 128), F32)],
            compiler_params=pltpu.CompilerParams(vmem_limit_bytes=vmem * MIB),
            cost_estimate=pl.CostEstimate(
                flops=int(cost * PACE * 1.15e9), bytes_accessed=int(cost * PACE * 3.69e6), transcendentals=0
            ),
            input_output_aliases={used + i: i for i in range(len(into))},
            name=name,
        )(*args, *deps)
        self.mark = got[-1]
        return got[:-1] if several else got[0]


def half_mask(head):
    return (lax.broadcasted_iota(jnp.int32, (1, 2 * HD), 1) // HD) == head


def causal_tile(blk):
    key = lax.broadcasted_iota(jnp.int32, (blk, blk), 0)
    return key <= lax.broadcasted_iota(jnp.int32, (blk, blk), 1)


def staged(work, *stages):
    first, second, third = stages
    ahead, behind = first(*work[0]), None
    for t in range(len(work) + 1):
        coming = first(*work[t + 1]) if t + 1 < len(work) else None
        now = second(*work[t], *ahead) if t < len(work) else None
        if behind is not None:
            third(*work[t - 1], *behind)
        ahead, behind = coming, now


def attend_forward_kernel(len_ref, q_ref, k_ref, v_ref, o_ref, lse_ref, ot_ref):
    rows = q_ref.shape[0]
    blk, half = 256, rows // 2
    bias = jnp.where(len_ref[0, 0] < rows, HIDDEN, 0.0).astype(F32)
    vt = v_ref[...].T
    causal = causal_tile(blk)

    def scores(head, i):
        q = jnp.where(half_mask(head), q_ref[i * blk : (i + 1) * blk], jnp.zeros((), BF))
        parts = []
        for j in range(i + 1):
            s = nt(k_ref[j * blk : (j + 1) * blk], q)
            if j == i:
                s = jnp.where(causal, s, HIDDEN)
            elif i * blk >= half and (j + 1) * blk <= half:
                s = s + bias
            parts.append(s)
        return (parts,)

    def weights(head, i, parts):
        m = functools.reduce(jnp.maximum, [s.max(axis=0, keepdims=True) for s in parts])
        total = jnp.zeros((1, blk), F32)
        probs = []
        for s in parts:
            p = jnp.exp(s - m)
            total = total + p.sum(axis=0, keepdims=True)
            probs.append(p.astype(BF))
        lse_ref[0, head : head + 1, i * blk : (i + 1) * blk] = m + jnp.log(total)
        return probs, total

    def mix(head, i, probs, total):
        hs = slice(HD * head, HD * head + HD)
        mixed = sum(nn(vt[hs, j * blk : (j + 1) * blk], p) for j, p in enumerate(probs))
        ot_ref[hs, i * blk : (i + 1) * blk] = mixed / total

    staged([(head, i) for i in range(rows // blk) for head in range(2)], scores, weights, mix)
    o_ref[...] = ot_ref[...].T.astype(BF)


def attend_forward(chain, lengths, q, k, v, first, count, into=None):
    rows, width = q.shape
    pair = pl.BlockSpec((rows, 2 * HD), lambda p: (0, p + first))
    return chain.call(
        attend_forward_kernel,
        (lengths, q, k, v),
        grid=(count,),
        in_specs=[SCALARS, pair, pair, pair],
        out_specs=[pair, pl.BlockSpec((1, 2, rows), lambda p: (p + first, 0, 0))],
        out_shape=[shape_of((rows, width)), shape_of((width // (2 * HD), 2, rows), F32)],
        scratch_shapes=[pltpu.VMEM((2 * HD, rows), F32)],
        into=into,
        vmem=VMEM,
        cost=3.5 * count,
        name="attend_forward",
    )


def attend_backward_kernel(
    len_ref, q_ref, k_ref, v_ref, o_ref, do_ref, lse_ref, dq_ref, dk_ref, *rest, first, fresh, parts
):
    dv_refs, (dqt_acc, dv_acc, dk_acc) = rest[:parts], rest[parts:]
    rows = q_ref.shape[0]
    blk, half = 256, rows // 2
    nb = rows // blk
    bias = jnp.where(len_ref[0, 0] < rows, HIDDEN, 0.0).astype(F32)
    prod = (do_ref[...].astype(F32) * o_ref[...].astype(F32)).T
    kt = k_ref[...].T
    causal = causal_tile(blk)
    delta = [prod[HD * h : HD * h + HD].sum(axis=0, keepdims=True) for h in range(2)]
    qh = [jnp.where(half_mask(h), q_ref[...], jnp.zeros((), BF)) for h in range(2)]
    doh = [jnp.where(half_mask(h), do_ref[...], jnp.zeros((), BF)) for h in range(2)]
    block = lambda i: slice(i * blk, (i + 1) * blk)
    sums = {}

    def scores(head, j, i):
        return nt(k_ref[block(j)], qh[head][block(i)]), nt(v_ref[block(j)], doh[head][block(i)])

    def weights(head, j, i, s, dp):
        if i == j:
            s = jnp.where(causal, s, HIDDEN)
        elif i * blk >= half and (j + 1) * blk <= half:
            s = s + bias
        p = jnp.exp(s - lse_ref[0, head : head + 1, block(i)])
        return p.astype(BF), (p * (dp - delta[head][:, block(i)])).astype(BF)

    def mix(head, j, i, p, ds):
        hs, at, kr = slice(HD * head, HD * head + HD), block(i), block(j)
        dv, dk = nn(p, doh[head][at]), nn(ds, qh[head][at])
        if i > j:
            dv, dk = sums[head, j][0] + dv, sums[head, j][1] + dk
        sums[head, j] = dv, dk
        dqt = nn(kt[hs, kr], ds)
        if j == 0:
            dqt_acc[hs, at] = dqt
        else:
            dqt_acc[hs, at] += dqt
        if i == nb - 1:
            dv, dk = sums.pop((head, j))
            if head == 0:
                dv_acc[kr] = dv
                dk_acc[kr] = dk
            else:
                dv_acc[kr] += dv
                dk_acc[kr] += dk

    staged([(h, j, i) for h in range(2) for j in range(nb) for i in range(j, nb)], scores, weights, mix)
    dq_ref[...] = (dqt_acc[...].T * 0.125).astype(BF)
    dk_ref[...] = dk_acc[...].astype(BF)
    dv = dv_acc[...].astype(BF)
    if len(dv_refs) == 1:
        dv_refs[0][...] = dv
        return
    pair = pl.program_id(0) + first

    @pl.when(pair < fresh)
    def _():
        dv_refs[0][...] = dv

    @pl.when(pair >= fresh)
    def _():
        dv_refs[1][...] = dv


def attend_backward(chain, lengths, q, k, v, o, do, lse, first, count, into=None, waits=()):
    rows, width = q.shape
    fresh = width // (4 * HD)
    pair = pl.BlockSpec((rows, 2 * HD), lambda p: (0, p + first))
    new = pl.BlockSpec((rows, 2 * HD), lambda p: (0, jnp.minimum(p + first, fresh - 1)))
    old = pl.BlockSpec((rows, 2 * HD), lambda p: (0, jnp.maximum(p + first - fresh, 0)))
    dvs = [new] * (first < fresh) + [old] * (first + count > fresh)
    return chain.call(
        functools.partial(attend_backward_kernel, first=first, fresh=fresh, parts=len(dvs)),
        (lengths, q, k, v, o, do, lse),
        grid=(count,),
        in_specs=[SCALARS] + [pair] * 5 + [pl.BlockSpec((1, 2, rows), lambda p: (p + first, 0, 0))],
        out_specs=[pair, pair] + dvs,
        out_shape=[shape_of((rows, width))] * 2 + [shape_of((rows, width // 2))] * len(dvs),
        scratch_shapes=[
            pltpu.VMEM((2 * HD, rows), F32),
            pltpu.VMEM((rows, 2 * HD), F32),
            pltpu.VMEM((rows, 2 * HD), F32),
        ],
        vmem=VMEM,
        cost=6 * count,
        into=into,
        waits=waits,
        name="attend_backward",
    )


def row_stats(v):
    center = v - jnp.mean(v, axis=-1, keepdims=True)
    rstd = lax.rsqrt(jnp.mean(center * center, axis=-1, keepdims=True) + EPSILON)
    return center * rstd, rstd


def norm_back(grad, unit, rstd, gain):
    g = grad * gain
    return rstd * (
        g - jnp.mean(g, axis=-1, keepdims=True) - unit * jnp.mean(g * unit, axis=-1, keepdims=True)
    )


def column_sum(v):
    return v.astype(F32).sum(axis=0, keepdims=True)


def clear(*refs):
    @pl.when(pl.program_id(0) == 0)
    def _():
        for r in refs:
            r[...] = jnp.zeros(r.shape, r.dtype)


def vector_parts(ref, d, vd):
    ff = ref.shape[1] - 7 * d - vd
    parts, at = [], 0
    for n in (d, d, d, vd, d, d, d, ff, d):
        parts.append(ref.at[:, at : at + n])
        at += n
    return parts


def project_kernel(*refs, pieces):
    if pieces:
        where_ref, *side = refs[: 2 * pieces + 1]
        x_ref, first_ref, vec_ref, a_ref, q_ref, k_ref, v_ref, w_ref, acc_ref = refs[2 * pieces + 1 :]

        @pl.when(pl.program_id(0) == 0)
        def _():
            load_side(where_ref, side[:pieces], side[pieces:], w_ref, acc_ref)
    else:
        x_ref, first_ref, vec_ref, w_ref, a_ref, q_ref, k_ref, v_ref = refs
    d, vd = x_ref.shape[1], first_ref.shape[1]
    g_ref, b_ref, bq_ref, bv_ref = vector_parts(vec_ref, d, vd)[:4]
    unit, _ = row_stats(x_ref[...].astype(F32))
    a = (unit * g_ref[...] + b_ref[...]).astype(BF)
    a_ref[...] = a
    q = (nn(a, w_ref[:, 0:d]) + bq_ref[...]).astype(BF)
    q_ref[...] = (q.astype(F32) * 0.125).astype(BF)
    k_ref[...] = nn(a, w_ref[:, d : 2 * d]).astype(BF)
    v_ref[:, 0:vd] = (nn(a, w_ref[:, 2 * d :]) + bv_ref[...]).astype(BF)
    v_ref[:, vd:] = first_ref[...]


def project(chain, x, first, vec, w, where=None, blk=256):
    rows, d = x.shape
    pieces = w is not None and where is not None
    args, specs = (x, first, vec), [rows_of(blk, d), rows_of(blk, first.shape[1]), whole(vec)]
    outs, shapes, scratch = [rows_of(blk, d)] * 4, [shape_of((rows, d))] * 4, []
    count = 0
    if pieces:
        own, sib = w
        count = len(own)
        _, r, n = own[0].shape
        n = n * (own[0].shape[0] // 4)
        args = (where, *own, *sib) + args
        specs = [SCALARS] + [kept(t) for t in (*own, *sib)] + specs
        outs = outs + [pl.BlockSpec((32 * r, n), lambda i: (0, 0))]
        shapes = shapes + [shape_of((32 * r, n))]
        scratch = [pltpu.VMEM((32 * r, n), F32)]
    else:
        args, specs = args + (w,), specs + [whole(w)]
    return chain.call(
        functools.partial(project_kernel, pieces=count),
        args,
        grid=(rows // blk,),
        in_specs=specs,
        out_specs=outs,
        out_shape=shapes,
        scratch_shapes=scratch,
        vmem=VMEM,
        cost=8,
        name="project",
    )


def feed_kernel(*refs, pieces, chunk=512):
    if pieces:
        where_ref, *side = refs[: pieces + 1]
        (
            o_ref, x_ref, c_ref, vec_ref, x1_ref, a_ref, y_ref, du_ref, dx_ref, dz_ref, do_ref,
            dbo_ref, dg_ref, db_ref, dbu_ref, dbd_ref, wd_ref, wo_ref, wu_ref, acc,
        ) = refs[pieces + 1 :]

        @pl.when(pl.program_id(0) == 0)
        def _():
            load_feed(where_ref, side[:4], side[4:8], side[8:10], side[10:], wu_ref, wd_ref, wo_ref, acc)
    else:
        (
            o_ref, x_ref, c_ref, vec_ref, wu_ref, wd_ref, wo_ref, x1_ref, a_ref, y_ref, du_ref, dx_ref,
            dz_ref, do_ref, dbo_ref, dg_ref, db_ref, dbu_ref, dbd_ref,
        ) = refs
    clear(dbo_ref, dg_ref, db_ref, dbu_ref, dbd_ref)
    d, ff = wu_ref.shape
    bo_ref, g_ref, b_ref, bu_ref = vector_parts(vec_ref, d, vec_ref.shape[1] - 7 * d - ff)[4:8]
    x1 = x_ref[...].astype(F32) + (nn(o_ref[...], wo_ref[...]) + bo_ref[...])
    x1_ref[...] = x1
    unit, rstd = row_stats(x1)
    a = (unit * g_ref[...] + b_ref[...]).astype(BF)
    a_ref[...] = a
    c = c_ref[...]
    da = jnp.zeros(x1.shape, F32)
    for s in range(0, wu_ref.shape[1], chunk):
        at = slice(s, s + chunk)
        u = nn(a, wu_ref[:, at]) + bu_ref[:, at]
        dy = nt(c, wd_ref[at])
        u2 = u * u
        t = jnp.tanh(u * (GELU + (GELU * CUBE) * u2))
        h = 0.5 * t + 0.5
        y_ref[:, at] = (u * h).astype(BF)
        slope = h + (0.5 * u) * (1.0 - t * t) * (GELU + (3 * GELU * CUBE) * u2)
        du = (slope * dy).astype(BF)
        du_ref[:, at] = du
        dbu_ref[:, at] += column_sum(du)
        da = da + nt(du, wu_ref[:, at])
    c32 = c.astype(F32)
    dbd_ref[...] += column_sum(c)
    db_ref[...] += column_sum(da)
    dg_ref[...] += column_sum(da * unit)
    dx = c32 + norm_back(da, unit, rstd, g_ref[...])
    dx_ref[...] = dx
    dz = dx.astype(BF)
    dz_ref[...] = dz
    dbo_ref[...] += column_sum(dz)
    do_ref[...] = nt(dz, wo_ref[...]).astype(BF)


def feed(chain, o, x, c, vec, weights, where=None, blk=256):
    rows, d = x.shape
    ff = vec.shape[1] - 7 * d - d // 2
    args = (o, x, c, vec)
    specs = [rows_of(blk, d)] * 3 + [whole(vec)]
    outs = [rows_of(blk, n) for n in (d, d, ff, ff, d, d, d)] + [vector_of(n) for n in (d, d, d, ff, d)]
    shapes = [
        shape_of((rows, d), F32), shape_of((rows, d)), shape_of((rows, ff)), shape_of((rows, ff)),
        shape_of((rows, d), F32), shape_of((rows, d)), shape_of((rows, d)),
    ] + [shape_of((1, n), F32) for n in (d, d, d, ff, d)]
    scratch, count = [], 0
    if where is not None:
        count = len(weights)
        args = (where, *weights) + args
        specs = [SCALARS] + [kept(t) for t in weights] + specs
        outs = outs + [pl.BlockSpec((ff, d), lambda i: (0, 0))]
        shapes = shapes + [shape_of((ff, d))]
        scratch = [pltpu.VMEM((d, d), BF), pltpu.VMEM((d, ff), BF), pltpu.VMEM((d, d), F32)]
    else:
        args, specs = args + tuple(weights), specs + [whole(t) for t in weights]
    return chain.call(
        functools.partial(feed_kernel, pieces=count),
        args,
        grid=(rows // blk,),
        in_specs=specs,
        out_specs=outs,
        out_shape=shapes,
        scratch_shapes=scratch,
        vmem=VMEM,
        cost=31,
        name="feed_forward",
    )


def output_kernel(y_ref, x1_ref, vec_ref, wd_ref, out_ref, acc_ref):
    step = pl.program_id(0)

    @pl.when(step == 0)
    def _():
        acc_ref[...] = x1_ref[...] + vec_ref[:, vec_ref.shape[1] - x1_ref.shape[1] :]

    acc_ref[...] += nn(y_ref[...], wd_ref[...])

    @pl.when(step == pl.num_programs(0) - 1)
    def _():
        out_ref[...] = acc_ref[...].astype(BF)


def final_output(chain, y, x1, vec, wd, part=0, parts=1, into=None, waits=(), blk=768):
    rows, ff = y.shape[0] // parts, y.shape[1]
    d = x1.shape[1]
    return chain.call(
        output_kernel,
        (y, x1, vec, wd),
        grid=(ff // blk,),
        in_specs=[
            pl.BlockSpec((rows, blk), lambda i: (part, i)),
            pl.BlockSpec((rows, d), lambda i: (part, 0), pipeline_mode=pl.Buffered(1)),
            whole(vec),
            rows_of(blk, d),
        ],
        out_specs=pl.BlockSpec((rows, d), lambda i: (part, 0)),
        out_shape=shape_of(x1.shape),
        into=into,
        scratch_shapes=[pltpu.VMEM((rows, d), F32)],
        waits=waits,
        vmem=VMEM,
        cost=8,
        name="output",
    )


def input_kernel(
    where_ref, dq_ref, dk_ref, df_ref, w_ref, x_ref, dx_ref, vec_ref,
    dbo_ref, dg2_ref, db2_ref, dbu_ref, dbd_ref, gt_ref, *rest, split,
):
    dvec_ref = rest[-1]
    clear(dvec_ref)
    half = df_ref.shape[1]
    d = x_ref.shape[1]
    dg, db, dbq, dbv, dbo, dg2, db2, dbu, dbd = vector_parts(dvec_ref, d, half)
    dq, dk, df = dq_ref[...], dk_ref[...], df_ref[...]
    da = nt(dq, w_ref[:, 0:d]) + nt(dk, w_ref[:, d : 2 * d]) + nt(df, w_ref[:, 2 * d :])
    dbq[...] += column_sum(dq)
    dbv[...] += column_sum(df)
    unit, rstd = row_stats(x_ref[...].astype(F32))
    db[...] += column_sum(da)
    dg[...] += column_sum(da * unit)
    gt_ref[...] = (dx_ref[...] + norm_back(da, unit, rstd, vec_ref[:, 0:d])).astype(BF)

    @pl.when(pl.program_id(0) == pl.num_programs(0) - 1)
    def _():
        for ref, known in ((dbo, dbo_ref), (dg2, dg2_ref), (db2, db2_ref), (dbu, dbu_ref), (dbd, dbd_ref)):
            ref[...] = known[...]
        if not split:
            rest[0][...] = dvec_ref[...]
            return
        plane, core = where_ref[1], where_ref[2]
        n = rest[0].shape[1]
        parts = [dvec_ref[:, f * n : (f + 1) * n] for f in range(8)]
        for side, out in enumerate(rest[:2]):
            for r in range(4):
                f = jnp.bitwise_xor(plane, r) * 2 + (core if side == 0 else 1 - core)
                v = parts[0]
                for g in range(1, 8):
                    v = jnp.where(f == g, parts[g], v)
                out[r : r + 1, :] = v


def input_grad(chain, where, terms, w, x, dx, vec, known, split, waits=(), blk=256):
    rows, d = x.shape
    n = vec.shape[1]
    vecs = [(4, n // 8)] * 2 if split else [(1, n)]
    return chain.call(
        functools.partial(input_kernel, split=split),
        (where, *terms, w, x, dx, vec, *known),
        grid=(rows // blk,),
        in_specs=[SCALARS] + [rows_of(blk, t.shape[1]) for t in terms] + [whole(w), rows_of(blk, d), rows_of(blk, d)]
        + [whole(t) for t in (vec, *known)],
        out_specs=[rows_of(blk, d)] + [pl.BlockSpec(t, lambda i: (0, 0)) for t in vecs],
        out_shape=[shape_of((rows, d))] + [shape_of(t, F32) for t in vecs],
        scratch_shapes=[pltpu.VMEM((1, n), F32)],
        waits=waits,
        vmem=VMEM,
        cost=9,
        name="input_grad",
    )


def flipped(r):
    return 2 * lax.rem(r, 2) + lax.div(r, 2)


def gathered_slot(r, core):
    return jnp.where(core == 0, r, flipped(r))


def summed_slot(r, core):
    return jnp.where(core == 0, flipped(r), r)


def plane_step(v, step):
    return lax.ppermute(v, "fsdp", [(i, i ^ (2 if i % 2 == step else 4)) for i in range(8)])


def depth_step(v, step):
    pairs = [(i, i ^ (8 if i % 2 == step else 16)) for i in range(32)]
    return lax.ppermute(v, AXES, pairs)


def depth_swap(v, bits):
    return lax.ppermute(v, "dp", [(i, i ^ bits) for i in range(4)])


def fsdp_swap(v, bit):
    return lax.ppermute(v, "fsdp", [(i, i ^ bit) for i in range(8)])


def core_step(v):
    return fsdp_swap(v, 1)


def resident(a):
    return pl.BlockSpec(a.shape, lambda *at: (0,) * a.ndim)


def pack(chain, parts, vec, n):
    rows, columns = parts[0].shape[1:]
    each = columns // n
    m = vec.shape[1]

    def kernel(*refs):
        v_ref, out, acc = refs[len(parts) :]
        at = 0
        for ref in refs[: len(parts)]:
            for i in range(ref.shape[0]):
                for c in range(each):
                    out[at] = ref[i, :, c * n : (c + 1) * n]
                    at += 1
        acc[...] = jnp.zeros(acc.shape, F32)
        for row, lane in enumerate(range(0, m, n)):
            rest = v_ref[:, lane : min(lane + n, m)]
            for term in range(3):
                part = rest.astype(BF).astype(F32)
                acc[3 * term + row : 3 * term + row + 1, 0 : part.shape[1]] = part
                rest = rest - part
        out[at] = acc[...].astype(BF)

    shape = shape_of((each * sum(p.shape[0] for p in parts) + 1, rows, n))
    return chain.call(
        kernel,
        (*parts, vec),
        grid=(1,),
        in_specs=[resident(p) for p in (*parts, vec)],
        out_specs=resident(shape),
        out_shape=shape,
        scratch_shapes=[pltpu.VMEM((rows, n), F32)],
        vmem=8,
        cost=1,
        name="pack",
    )


def places(where_ref, own, sib, straight=False):
    z, plane, core = where_ref[0], where_ref[1], where_ref[2]
    for side, group in enumerate((own, sib)):
        half = core if side == 0 else 1 - core
        for rp, ref in enumerate(group):
            for t in range(4):
                rz = t if straight else gathered_slot(t, half)
                chip = jnp.bitwise_xor(z, rz) * 4 + jnp.bitwise_xor(plane, gathered_slot(rp, half))
                yield ref, t, chip * 2 + half


def load_side(where_ref, own, sib, out, acc):
    rows, n = own[0].shape[1:]
    each = out.shape[1] // n
    for ref, t, device in places(where_ref, own, sib, True):
        at = pl.ds(pl.multiple_of(device * rows, 8), rows)
        for c in range(each):
            acc[at, c * n : (c + 1) * n] = ref[t * each + c].astype(F32)
    out[...] = acc[...].astype(BF)


def load_feed(where_ref, own, sib, own_d, sib_d, wu, wd, wo, acc):
    rows, n = own[0].shape[2:]
    wide = wu.shape[1] // n
    tall = wd.shape[0] // 32
    at = lambda device: pl.ds(pl.multiple_of(device * rows, 8), rows)
    before = {id(ref): d for ref, d in zip((*own, *sib), [(own_d, r) for r in range(4)] + [(sib_d, r) for r in range(4)])}
    for ref, t, device in places(where_ref, own, sib):
        group, rp = before[id(ref)]
        early = group[t // 2]
        parts = [early[t % 2, rp, q] for q in range(early.shape[2])]
        parts += [ref[t, q] for q in range(wide + 1, ref.shape[1])]
        part = jnp.concatenate([p.astype(F32) for p in parts], axis=0)
        wd[pl.ds(pl.multiple_of(device * tall, tall), tall), :] = part.astype(BF)
        acc[at(device), :] = ref[t, wide].astype(F32)
    wo[...] = acc[...].astype(BF)
    for c in range(wide):
        for ref, t, device in places(where_ref, own, sib):
            acc[at(device), :] = ref[t, c].astype(F32)
        wu[:, c * n : (c + 1) * n] = acc[...].astype(BF)


class Sum:
    def __init__(self, own, sib):
        self.own = own
        self.got = tuple(core_step(t) for t in sib)

    def start(self):
        self.terms = [self.own[0], self.got[0]]
        return (self.own[1].astype(F32) + self.got[1].astype(F32)).astype(BF)

    def upper(self, got):
        self.terms.append(got)
        n = got.shape[0]
        return sum(t[n // 2 : n].astype(F32) for t in self.terms).astype(BF)

    def total(self, got, part):
        return sum(t[0, part].astype(F32) for t in self.terms + [got])


def hand_out(where_ref, acc, piece, own, sib, depth_first):
    z, plane, core = where_ref[0], where_ref[1], where_ref[2]
    for refs, half in ((own, core), (sib, 1 - core)):
        for slot in range(16):
            z_slot, p_slot = (slot // 4, slot % 4) if depth_first else (slot % 4, slot // 4)
            pd = jnp.bitwise_xor(plane, summed_slot(p_slot, half))
            zd = jnp.bitwise_xor(z, summed_slot(z_slot, half))
            row = pl.multiple_of(((zd * 4 + pd) * 2 + half) * piece, 8)
            refs[slot // 8][slot % 8, 0] = acc[pl.ds(row, piece)].astype(BF)


def wide_grad(chain, where, left, rights, blk, name, depth_first=False, waits=()):
    rows, m = left.shape
    piece = m // 32
    starts, steps = [], 0
    for r in rights:
        starts.append(steps)
        steps += r.shape[1] // blk

    def kernel(where_ref, l_ref, *refs):
        r_refs, (own_lo, own_hi, sib_lo, sib_hi, lt_ref, r_all, acc) = refs[: len(rights)], refs[len(rights) :]
        step = pl.program_id(0)

        @pl.when(step == 0)
        def _():
            lt_ref[...] = l_ref[...].T

        if len(rights) == 1:
            right = r_refs[0][...]
        else:
            for ref, start, end in zip(r_refs, starts, starts[1:] + [steps]):

                @pl.when((step >= start) & (step < end))
                def _(ref=ref):
                    r_all[...] = ref[...]

            right = r_all[...]
        acc[...] = nn(lt_ref[...], right)
        hand_out(where_ref, acc, piece, (own_lo, own_hi), (sib_lo, sib_hi), depth_first)

    def chunk(r, start):
        n = r.shape[1] // blk
        return pl.BlockSpec((rows, blk), lambda i: (0, jnp.clip(i - start, 0, n - 1)))

    block = pl.BlockSpec((8, 1, piece, blk), lambda i: (0, i, 0, 0))
    own_lo, own_hi, sib_lo, sib_hi = chain.call(
        kernel,
        (where, left, *rights),
        grid=(steps,),
        in_specs=[SCALARS, whole(left)] + [chunk(r, start) for r, start in zip(rights, starts)],
        out_specs=[block] * 4,
        out_shape=[shape_of((8, steps, piece, blk))] * 4,
        scratch_shapes=[pltpu.VMEM((m, rows), BF), pltpu.VMEM((rows, blk), BF), pltpu.VMEM((m, blk), F32)],
        waits=waits,
        vmem=VMEM,
        cost=9,
        name=name,
    )
    return (own_lo, own_hi), (sib_lo, sib_hi)


def tall_grad_kernel(
    where_ref, y_ref, c_ref, o_ref, dz_ref, own_lo, own_hi, sib_lo, sib_hi, acc_ref, out_ref
):
    step = pl.program_id(0)
    tall = y_ref.shape[1] // 8
    flat = o_ref.shape[1] // 32

    @pl.when(step == 0)
    def _():
        out_ref[...] = tn(o_ref[...], dz_ref[...])

    acc_ref[...] = tn(y_ref[...], c_ref[...])
    plane, core = where_ref[1], where_ref[2]
    for refs, half in (((own_lo, own_hi), core), ((sib_lo, sib_hi), 1 - core)):
        for slot in range(4):
            near = jnp.bitwise_xor(plane, summed_slot(slot, half)) * 2 + half
            out = refs[slot // 2]
            for q in range(tall // flat):
                row = pl.multiple_of(near * tall + q * flat, 8)
                out[slot % 2, 0, q] = acc_ref[pl.ds(row, flat)].astype(BF)
            row = pl.multiple_of((step * 8 + near) * flat, 8)
            out[slot % 2, 0, tall // flat] = out_ref[pl.ds(row, flat)].astype(BF)


def tall_grad(chain, where, y, c, o, dz):
    rows, ff = y.shape
    d = c.shape[1]
    piece = d // 32
    chunks = ff // d + 1

    def slot(flip):
        def index(i, where_ref):
            core = where_ref[2]
            return (0, summed_slot(jnp.bitwise_xor(i, where_ref[0]), 1 - core if flip else core), 0, 0, 0)

        return pl.BlockSpec((2, 1, chunks, piece, d), index)

    got = chain.call(
        tall_grad_kernel,
        (where, y, c, o, dz),
        scalars=1,
        grid=(4,),
        in_specs=[pl.BlockSpec((rows, ff // 4), lambda i, w: (0, i)), kept(c), kept(o), kept(dz)],
        out_specs=[slot(False), slot(False), slot(True), slot(True)],
        out_shape=[shape_of((2, 4, chunks, piece, d))] * 4,
        scratch_shapes=[pltpu.VMEM((ff // 4, d), F32), pltpu.VMEM((d, d), F32)],
        vmem=VMEM,
        cost=12.5,
        name="down_out_grad",
    )
    own_lo, own_hi, sib_lo, sib_hi = (t.reshape(8, chunks, piece, d) for t in got)
    return (own_lo, own_hi), (sib_lo, sib_hi)


def arrange_vectors(chain, where, own, sib, m):
    last, rows, n = own[0].shape

    def kernel(where_ref, *refs):
        plane, core = where_ref[1], where_ref[2]
        out = refs[8]
        found = []
        for ref in refs[:8]:
            t = ref[0].astype(F32)
            found.append(t[0:3] + t[3:6] + t[6:9])
        for f in range(8):
            mine = core == f % 2
            slot = gathered_slot(jnp.bitwise_xor(plane, f // 2), f % 2)
            v = jnp.where(mine, found[0], found[4])
            for r in range(1, 4):
                v = jnp.where(slot == r, jnp.where(mine, found[r], found[4 + r]), v)
            for row, at in enumerate(range(0, m, n)):
                w = min(n, m - at)
                out[:, f * m + at : f * m + at + w] = v[row : row + 1, 0:w]

    block = pl.BlockSpec((1, rows, n), lambda i: (last - 1, 0, 0))
    return chain.call(
        kernel,
        (where, *own, *sib),
        grid=(1,),
        in_specs=[SCALARS] + [block] * 8,
        out_specs=vector_of(8 * m),
        out_shape=shape_of((1, 8 * m), F32),
        vmem=8,
        cost=1,
        name="arrange_vectors",
    )


def after(values, *deps):
    return lax.optimization_barrier((values, deps))[0]


def whole_gather(w, axes=AXES):
    return lax.all_gather(w, axes, axis=0, tiled=True)


def general(tokens, first_values, cotangent, lengths, vectors, w_qkv, w_out, w_up, w_down):
    d = tokens.shape[1]
    chain = Chain()
    scatter = lambda g: lax.psum_scatter(g, AXES, scatter_dimension=0, tiled=True)
    vec = whole_gather(vectors, "fsdp").reshape(1, -1)
    f_qkv, f_out, f_up, f_down = (whole_gather(w) for w in (w_qkv, w_out, w_up, w_down))
    where = jnp.zeros((3,), jnp.int32)
    a1, q, k, v = project(chain, tokens, first_values, vec, f_qkv)
    n = d // (4 * HD)
    o, lse = attend_forward(chain, lengths, q, k, v, 0, 2 * n)
    x1, a2, y, du, dx1, dz, do, *known = feed(chain, o, tokens, cotangent, vec, (f_up, f_down, f_out))
    output = final_output(chain, y, x1, vec, f_down)
    dq, dk, df, dfirst = attend_backward(chain, lengths, q, k, v, o, do, lse, 0, 2 * n)
    terms = (dq, dk, df)
    grad_tokens, dvec = input_grad(chain, where, terms, f_qkv, tokens, dx1, vec, known, False)
    n = vectors.shape[0]
    grad_vectors = lax.dynamic_slice_in_dim(lax.psum(dvec[0], AXES), lax.axis_index("fsdp") * n, n, 0)
    return (
        output, grad_tokens, dfirst, grad_vectors,
        scatter(tn(a1, jnp.concatenate(terms, axis=1))), scatter(tn(o, dz)), scatter(tn(a2, du)), scatter(tn(y, cotangent)),
    )


def local(tokens, first_values, cotangent, lengths, vectors, w_qkv, w_out, w_up, w_down):
    d = tokens.shape[1]
    index = lax.axis_index("fsdp")
    plane, core = lax.div(index, 2), lax.rem(index, 2)
    where = jnp.stack([lax.axis_index("dp"), plane, core]).astype(jnp.int32)
    piece = w_qkv.shape[0]
    tall = w_down.shape[0] // piece
    chain = Chain()

    grow = lambda a, b: jnp.concatenate([a, b], axis=0)
    chunks = w_down.reshape(tall, piece, d)
    early = chunks[: tall // 2][None]
    late = jnp.concatenate([w_up.reshape(piece, -1, d).transpose(1, 0, 2), w_out[None], chunks[tall // 2 :]], axis=0)[None]
    m = [w_qkv[None]] + [depth_swap(w_qkv[None], bits) for bits in (1, 2, 3)]
    m, near_e, side_e, early, late = after((m, plane_step(early, 0), plane_step(early, 1), early, late))

    m = pack(chain, m, vectors[None], d // 2)
    near, side = plane_step(m, 0), plane_step(m, 1)
    far_e, got = plane_step(near_e, 1), depth_step(late, 0)
    m, near, side, far_e, late, got = after((m, near, side, far_e, late, got))

    late = grow(late, got)
    early = jnp.concatenate([early, near_e, side_e, far_e], axis=0)[None]
    far, sib, got = plane_step(near, 1), core_step(m), depth_step(late, 1)
    far, sib, got, late, early = after((far, sib, got, late, early))

    late = grow(late, got)
    own, sib = [m, near, side, far], [sib] + [core_step(t) for t in (near, side, far)]
    near_l, side_l, got = plane_step(late, 0), plane_step(late, 1), depth_step(early, 0)
    vec = arrange_vectors(chain, where, own, sib, vectors.shape[0])
    a1, q, k, v, f_qkv = project(chain, tokens, first_values, vec, (own, sib), where)
    early, got, late, near_l, side_l = after((early, got, late, near_l, side_l), a1)

    early = grow(early, got)
    got, sib_e = depth_step(early, 1), [core_step(early)]
    far_l = plane_step(near_l, 1)
    sib_l = [core_step(t) for t in (late, near_l, side_l)]
    o, lse = attend_forward(chain, lengths, q, k, v, 0, 6)
    far_l, sib_l, got = after((far_l, sib_l, got), o)
    sib_l += [core_step(far_l)]
    sib_e += [core_step(got)]
    x1, a2, y, du, dx1, dz, do, *known, f_down = feed(
        chain, o, tokens, cotangent, vec,
        (late, near_l, side_l, far_l, *sib_l, early, got, *sib_e), where,
    )

    sum_d = Sum(*tall_grad(chain, where, y, cotangent, o, dz))
    sum_u = Sum(*wide_grad(chain, where, a2, [du], d, "up_grad", True))
    sum_d.got = after(sum_d.got, sum_u.own)
    send_d, send_u = sum_d.start(), sum_u.start()
    got_d, got_u = plane_step(send_d, 0), depth_step(send_u, 0)
    dq, dk, df, dfirst = attend_backward(chain, lengths, q, k, v, o, do, lse, 0, d // (2 * HD), None, (send_d, send_u))
    terms = (dq, dk, df)
    sum_q = Sum(*wide_grad(chain, where, a1, terms, d // 2, "qkv_grad"))
    got_d, got_u = after((got_d, got_u), sum_q.own)
    send_d, send_u = sum_d.upper(got_d), sum_u.upper(got_u)
    got_d, got_u = plane_step(send_d, 1), depth_step(send_u, 1)
    sum_q.got = after(sum_q.got, send_d, send_u)
    send_q = sum_q.start()
    got_q = plane_step(send_q, 0)
    grad_tokens, vec_own, vec_sib = input_grad(
        chain, where, terms, f_qkv, tokens, dx1, vec, known, True, (send_q, send_d, send_u)
    )
    got_q, got_d, got_u, vec_sib = after((got_q, got_d, got_u, vec_sib))
    send_q = sum_q.upper(got_q)
    got_q, got_vec = plane_step(send_q, 1), core_step(vec_sib)
    got_d, got_u = after((got_d, got_u), send_q)
    send_d, send_u = sum_d.upper(got_d), sum_u.upper(got_u)
    got_d, got_u = depth_step(send_d, 0), plane_step(send_u, 0)
    output = final_output(chain, y, x1, vec, f_down, 0, 1, None, (send_q, send_d, send_u))
    got_q, got_d, got_u, got_vec = after((got_q, got_d, got_u, got_vec), output)
    send_q = sum_q.upper(got_q)
    got_d, got_u, got_vec = after((got_d, got_u, got_vec), send_q)
    got_q = depth_step(send_q, 0)
    got_d, got_u = depth_step(sum_d.upper(got_d), 1), plane_step(sum_u.upper(got_u), 1)
    v = vec_own + got_vec
    got_vec = [fsdp_swap(v[bits], 2 * bits) for bits in (1, 2, 3)]
    send_q = sum_q.upper(got_q)
    got_vec = after(got_vec, send_q)
    got_q = depth_step(send_q, 1)
    got_d, got_u = after((got_d, got_u), send_q)
    v = v[0] + sum(got_vec)
    grad_vectors = v + sum(depth_swap(v, bits) for bits in (1, 2, 3))
    grad_down, grad_out = sum_d.total(got_d, slice(0, tall)).reshape(tall * piece, d), sum_d.total(got_d, tall)
    wide = lambda t: t.transpose(1, 0, 2).reshape(piece, -1)
    grad_up = wide(sum_u.total(got_u, slice(None)))
    grad_qkv = wide(sum_q.total(got_q, slice(None)))
    return output, grad_tokens, dfirst, grad_vectors, grad_qkv, grad_out, grad_up, grad_down


def solution(mesh):
    rows = P(AXES, None)
    small = mesh.shape["dp"] == 4 and mesh.shape["fsdp"] == 8
    return jax.shard_map(
        local if small else general,
        mesh=mesh,
        in_specs=(rows, rows, rows, rows, P("fsdp"), rows, rows, rows, rows),
        out_specs=(rows, rows, rows, P("fsdp"), rows, rows, rows, rows),
        check_vma=False,
    )
```

profile of v0, /device:TPU:0, one launch (start us, length us, event | category | flops | bytes accessed | tf_op | source)
XLA Modules:
  0.0 259.1 jit_solution(6642312005927350179)
XLA Ops:
  0.6 5.1 %collective-permute-start.2 = (bf16[1,24,1920]{2,1,0:T(8,128)(2,1)}, bf16[1,24,1920]{2,1,0:T(8,128)(2,1)S(1)}, u32[]{:S(2)}, u32[]{:S(2)}) collective-permute-start(bf16[1,24,1920]{2,1,0:T(8,128)(2,1)} %bitcast.42), channel_id=1, source_target_pairs={{0,24},{8,16},{16,8},{24,0},{1,25},{9,17},{17,9},{25,1},{2,26},{10... | collective-permute-start | bytes 276488 | tf_op jit(solution)/shard_map/ppermute | solution.py:560
  7.3 1.7 collective-permute-start.4
  9.1 1.5 collective-permute-start.3
  14.7 1.6 collective-permute-start.6
  16.3 1.5 collective-permute-start.5
  19.2 7.6 %collective-permute-done.7 = bf16[1,2,24,768]{3,2,1,0:T(8,128)(2,1)S(1)} collective-permute-done((bf16[1,2,24,768]{3,2,1,0:T(8,128)(2,1)S(1)}, bf16[1,2,24,768]{3,2,1,0:T(8,128)(2,1)S(1)}, u32[]{:S(2)}, u32[]{:S(2)}) %collective-permute-start.7) | collective-permute-done | bytes 73760 | tf_op jit(solution)/shard_map/ppermute | solution.py:551
  29.2 6.0 %collective-permute-done.9.refs_4_ = bf16[21,24,384]{2,1,0:T(8,128)(2,1)S(1)} collective-permute-done((bf16[21,24,384]{2,1,0:T(8,128)(2,1)S(1)}, bf16[21,24,384]{2,1,0:T(8,128)(2,1)S(1)}, u32[]{:S(2)}, u32[]{:S(2)}) %collective-permute-start.9) | collective-permute-done | bytes 387104 | tf_op jit(solution)/shard_map/ppermute | solution.py:551
  35.2 7.2 %collective-permute-done.11 = bf16[2,7,24,768]{3,2,1,0:T(8,128)(2,1)S(1)} collective-permute-done((bf16[2,7,24,768]{3,2,1,0:T(8,128)(2,1)S(1)}, bf16[2,7,24,768]{3,2,1,0:T(8,128)(2,1)S(1)}, u32[]{:S(2)}, u32[]{:S(2)}) %collective-permute-start.11) | collective-permute-done | bytes 516128 | tf_op jit(solution)/shard_map/ppermute | solution.py:556
  44.1 1.5 collective-permute-start.14
  46.7 1.2 collective-permute-done.16.refs_7_
  50.9 9.6 %project.1 = (bf16[1024,768]{1,0:T(8,128)(2,1)}, bf16[1024,768]{1,0:T(8,128)(2,1)}, bf16[1024,768]{1,0:T(8,128)(2,1)}, bf16[1024,768]{1,0:T(8,128)(2,1)}, bf16[768,1920]{1,0:T(8,128)(2,1)}, /*index=5*/f32[8,128]{1,0:T(8,128)}) custom-call(s32[3]{0:T(128)} %copy-done.10, bf16[21,24,384]{2,1,0:T(8,128)(2,1)} %copy-done, bf16[21,24,384]{2,1,0:T(8,128)(2,1)} %copy-done.2, ...), custom_call_target="tpu_custom_call" | custom-call | flops 92000000 | bytes 295200 | tf_op jit(solution)/shard_map/project/pallas_call | solution.py:80
  60.5 2.3 collective-permute-done.14.refs_3_
  63.3 1.7 collective-permute-start.18
  66.0 1.3 collective-permute-start.22
  67.3 13.8 %attend_forward.1 = (bf16[1024,768]{1,0:T(8,128)(2,1)}, f32[6,2,1024]{2,1,0:T(2,128)}, f32[8,128]{1,0:T(8,128)}) custom-call(s32[1,2]{1,0:T(1,128)} %refs_0_.3, bf16[1024,768]{1,0:T(8,128)(2,1)} %get-tuple-element.142.refs_1_, bf16[1024,768]{1,0:T(8,128)(2,1)} %get-tuple-element.143.refs_2_, bf16[1024,768]{1,0:T(8,128)(2,1)} %get-tuple-element.144.refs_3_, ...), custom_call_target="tpu_custom_call" | custom-call | flops 241500000 | bytes 774900 | tf_op jit(solution)/shard_map/attend_forward/pallas_call | solution.py:80
  81.2 2.2 collective-permute-done.22.refs_10_
  84.1 3.4 %collective-permute-done.24.refs_11_ = bf16[2,4,2,24,768]{4,3,2,1,0:T(8,128)(2,1)S(1)} collective-permute-done((bf16[2,4,2,24,768]{4,3,2,1,0:T(8,128)(2,1)S(1)}, bf16[2,4,2,24,768]{4,3,2,1,0:T(8,128)(2,1)S(1)}, u32[]{:S(2)}, u32[]{:S(2)}) %collective-permute-start.24) | collective-permute-done | bytes 589856 | tf_op jit(solution)/shard_map/ppermute | solution.py:564
  89.1 35.6 %feed_forward.1 = (f32[1024,768]{1,0:T(8,128)}, bf16[1024,768]{1,0:T(8,128)(2,1)}, bf16[1024,3072]{1,0:T(8,128)(2,1)}, bf16[1024,3072]{1,0:T(8,128)(2,1)}, f32[1...) custom-call(s32[3]{0:T(128)} %copy-done.10, ...), custom_call_target="tpu_custom_call" | custom-call | flops 356500000 | bytes 1143900 | tf_op jit(solution)/shard_map/feed_forward/pallas_call | solution.py:80
  124.6 13.2 %down_out_grad.1 = (bf16[2,4,5,24,768]{4,3,2,1,0:T(8,128)(2,1)}, bf16[2,4,5,24,768]{4,3,2,1,0:T(8,128)(2,1)}, bf16[2,4,5,24,768]{4,3,2,1,0:T(8,128)(2,1)}, bf16[2,4,5,24,768]{4,3,2,1,0:T(8,128)(2,1)}, f32[8,128]{1,0:T(8,128)}) custom-call(s32[3]{0:T(128)} %copy-done.10, bf16[1024,3072]{1,0:T(8,128)(2,1)} %get-tuple-element.153.refs_1_.refs_0_, ...), custom_call_target="tpu_custom_call" | custom-call | flops 143750000 | bytes 461250 | tf_op jit(solution)/shard_map/down_out_grad/pallas_call | solution.py:80
  138.4 9.9 %up_grad.1 = (bf16[8,4,24,768]{3,2,1,0:T(8,128)(2,1)}, bf16[8,4,24,768]{3,2,1,0:T(8,128)(2,1)}, bf16[8,4,24,768]{3,2,1,0:T(8,128)(2,1)}, bf16[8,4,24,768]{3,2,1,0:T(8,128)(2,1)}, f32[8,128]{1,0:T(8,128)}) custom-call(s32[3]{0:T(128)} %copy-done.10, bf16[1024,768]{1,0:T(8,128)(2,1)} %get-tuple-element.158.refs_1_, ...), custom_call_target="tpu_custom_call" | custom-call | flops 103500000 | bytes 332100 | tf_op jit(solution)/shard_map/up_grad/pallas_call | solution.py:80
  148.7 1.2 copy-done.19
  149.9 2.3 fusion.refs_8_
  152.2 1.8 collective-permute-start.31
  155.5 23.6 %attend_backward.1 = (bf16[1024,768]{1,0:T(8,128)(2,1)}, bf16[1024,768]{1,0:T(8,128)(2,1)}, bf16[1024,384]{1,0:T(8,128)(2,1)}, bf16[1024,384]{1,0:T(8,128)(2,1)}, f32[8,128]{1,0:T(8,128)}) custom-call(s32[1,2]{1,0:T(1,128)} %refs_0_.3, bf16[1024,768]{1,0:T(8,128)(2,1)} %get-tuple-element.142.refs_1_, bf16[1024,768]{1,0:T(8,128)(2,1)} %get-tuple-element.143.refs_2_, ...), custom_call_target="tpu_custom_call" | custom-call | flops 414000000 | bytes 1328400 | tf_op jit(solution)/shard_map/attend_backward/pallas_call | solution.py:80
  179.1 9.6 %qkv_grad.1 = (bf16[8,5,24,384]{3,2,1,0:T(8,128)(2,1)}, bf16[8,5,24,384]{3,2,1,0:T(8,128)(2,1)}, bf16[8,5,24,384]{3,2,1,0:T(8,128)(2,1)}, bf16[8,5,24,384]{3,2,1,0:T(8,128)(2,1)}, f32[8,128]{1,0:T(8,128)}) custom-call(s32[3]{0:T(128)} %copy-done.10, bf16[1024,768]{1,0:T(8,128)(2,1)} %get-tuple-element.136.refs_1_, ...), custom_call_target="tpu_custom_call" | custom-call | flops 103500000 | bytes 332100 | tf_op jit(solution)/shard_map/qkv_grad/pallas_call | solution.py:80
  189.3 1.6 add_convert_fusion.2.refs_16_
  190.9 1.8 fusion.2.refs_15_
  194.5 2.1 collective-permute-start.36
  196.6 10.2 %input_grad.1 = (bf16[1024,768]{1,0:T(8,128)(2,1)}, f32[4,1104]{1,0:T(4,128)}, f32[4,1104]{1,0:T(4,128)}, f32[8,128]{1,0:T(8,128)}) custom-call(s32[3]{0:T(128)} %copy-done.10, bf16[1024,768]{1,0:T(8,128)(2,1)} %get-tuple-element.171.refs_2_.refs_1_, bf16[1024,768]{1,0:T(8,128)(2,1)} %get-tuple-element.172.refs_3_.refs_2_, ...), custom_call_target="tpu_custom_call" | custom-call | flops 103500000 | bytes 332100 | tf_op jit(solution)/shard_map/input_grad/pallas_call | solution.py:80
  206.8 4.9 %collective-permute-done.36 = bf16[4,4,24,768]{3,2,1,0:T(8,128)(2,1)S(1)} collective-permute-done((bf16[4,4,24,768]{3,2,1,0:T(8,128)(2,1)S(1)}, bf16[4,4,24,768]{3,2,1,0:T(8,128)(2,1)S(1)}, u32[]{:S(2)}, u32[]{:S(2)}) %collective-permute-start.36) | collective-permute-done | bytes 589856 | tf_op jit(solution)/shard_map/ppermute | solution.py:556
  211.7 1.5 add_convert_fusion.4.refs_5_
  213.2 1.4 collective-permute-start.37
  214.6 1.4 add_convert_fusion.3.refs_6_
  216.4 1.3 add_convert_fusion.5.refs_7_
  217.7 1.4 collective-permute-start.39
  219.2 10.3 %output.1 = (bf16[1024,768]{1,0:T(8,128)(2,1)}, f32[8,128]{1,0:T(8,128)}) custom-call(bf16[1024,3072]{1,0:T(8,128)(2,1)} %get-tuple-element.153.refs_1_.refs_0_, f32[1024,768]{1,0:T(8,128)} %get-tuple-element.154.refs_1_, f32[1,8832]{1,0:T(1,128)} %copy-done.8, bf16[3072,768]{1,0:T(8,128)(2,1)} %get-tuple-element.155.refs_3_, ...), custom_call_target="tpu_custom_call" | custom-call | flops 92000000 | bytes 295200 | tf_op jit(solution)/shard_map/output/pallas_call | solution.py:80
  229.6 1.3 add_convert_fusion.7
  230.9 1.7 collective-permute-start.44
  233.6 1.3 collective-permute-start.42
  234.9 1.3 collective-permute-start.41
  238.2 1.3 add_convert_fusion.6
  239.6 1.8 collective-permute-start.49
  242.5 1.6 collective-permute-start.47
  244.3 2.6 collective-permute-start.45
  246.9 1.6 collective-permute-done.49
  248.5 1.5 add_bitcast_fusion.2
  250.0 1.9 add_add_fusion
  254.4 2.9 %collective-permute-done.48 = bf16[1,5,24,384]{3,2,1,0:T(8,128)(2,1)S(1)} collective-permute-done((bf16[1,5,24,384]{3,2,1,0:T(8,128)(2,1)S(1)}, bf16[1,5,24,384]{3,2,1,0:T(8,128)(2,1)S(1)}, u32[]{:S(2)}, u32[]{:S(2)}) %collective-permute-start.48) | collective-permute-done | bytes 92192 | tf_op jit(solution)/shard_map/ppermute | solution.py:556
  (169 shorter events, 33.2 us)
Async XLA Ops:
  0.6 12.8 %collective-permute-start.2 = (bf16[1,24,1920]{2,1,0:T(8,128)(2,1)}, bf16[1,24,1920]{2,1,0:T(8,128)(2,1)S(1)}, u32[]{:S(2)}, u32[]{:S(2)}) collective-permute-start(bf16[1,24,1920]{2,1,0:T(8,128)(2,1)} %bitcast.42), channel_id=1, source_target_pairs={{0,24},{8,16},{16,8},{24,0},{1,25},{9,17},{17,9},{25,1},{2,26},{10... | collective-permute-start | bytes 276488 | tf_op jit(solution)/shard_map/ppermute | solution.py:560
  5.7 7.9 %collective-permute-start.1 = (bf16[1,24,1920]{2,1,0:T(8,128)(2,1)}, bf16[1,24,1920]{2,1,0:T(8,128)(2,1)S(1)}, u32[]{:S(2)}, u32[]{:S(2)}) collective-permute-start(bf16[1,24,1920]{2,1,0:T(8,128)(2,1)} %bitcast.43), channel_id=1, source_target_pairs={{0,16},{8,24},{16,0},{24,8},{1,17},{9,25},{17,1},{25,9},{2,18},{10... | collective-permute-start | bytes 276488 | tf_op jit(solution)/shard_map/ppermute | solution.py:560
  5.8 7.9 %collective-permute-start = (bf16[1,24,1920]{2,1,0:T(8,128)(2,1)}, bf16[1,24,1920]{2,1,0:T(8,128)(2,1)S(1)}, u32[]{:S(2)}, u32[]{:S(2)}) collective-permute-start(bf16[1,24,1920]{2,1,0:T(8,128)(2,1)} %bitcast.44), channel_id=1, source_target_pairs={{0,8},{8,0},{16,24},{24,16},{1,9},{9,1},{17,25},{25,17},{2,10},{10... | collective-permute-start | bytes 276488 | tf_op jit(solution)/shard_map/ppermute | solution.py:560
  7.3 5.6 %collective-permute-start.4 = (bf16[1,2,24,768]{3,2,1,0:T(8,128)(2,1)S(1)}, bf16[1,2,24,768]{3,2,1,0:T(8,128)(2,1)S(1)}, u32[]{:S(2)}, u32[]{:S(2)}) collective-permute-start(bf16[1,2,24,768]{3,2,1,0:T(8,128)(2,1)S(1)} %bitcast.51), channel_id=1, source_target_pairs={{0,4},{1,3},{2,6},{3,1},{4,0},{5,7},{6,2},{7,5},{8,12},{9,11},{10,... | collective-permute-start | bytes 221192 | tf_op jit(solution)/shard_map/ppermute | solution.py:551
  9.1 4.4 %collective-permute-start.3 = (bf16[1,2,24,768]{3,2,1,0:T(8,128)(2,1)S(1)}, bf16[1,2,24,768]{3,2,1,0:T(8,128)(2,1)S(1)}, u32[]{:S(2)}, u32[]{:S(2)}) collective-permute-start(bf16[1,2,24,768]{3,2,1,0:T(8,128)(2,1)S(1)} %bitcast.52), channel_id=1, source_target_pairs={{0,2},{1,5},{2,0},{3,7},{4,6},{5,1},{6,4},{7,3},{8,10},{9,13},{10,... | collective-permute-start | bytes 221192 | tf_op jit(solution)/shard_map/ppermute | solution.py:551
  14.7 12.1 %collective-permute-start.6 = (bf16[21,24,384]{2,1,0:T(8,128)(2,1)S(1)}, bf16[21,24,384]{2,1,0:T(8,128)(2,1)S(1)}, u32[]{:S(2)}, u32[]{:S(2)}) collective-permute-start(bf16[21,24,384]{2,1,0:T(8,128)(2,1)S(1)} %get-tuple-element.121.refs_1_), channel_id=1, source_target_pairs={{0,4},{1,3},{2,6},{3,1},{4,0},{5,7},{6,2},{7,5},{8,12},{9,11},{10,... | collective-permute-start | bytes 1161224 | tf_op jit(solution)/shard_map/ppermute | solution.py:551
  16.3 10.5 %collective-permute-start.5 = (bf16[21,24,384]{2,1,0:T(8,128)(2,1)S(1)}, bf16[21,24,384]{2,1,0:T(8,128)(2,1)S(1)}, u32[]{:S(2)}, u32[]{:S(2)}) collective-permute-start(bf16[21,24,384]{2,1,0:T(8,128)(2,1)S(1)} %get-tuple-element.121.refs_1_), channel_id=1, source_target_pairs={{0,2},{1,5},{2,0},{3,7},{4,6},{5,1},{6,4},{7,3},{8,10},{9,13},{10,... | collective-permute-start | bytes 1161224 | tf_op jit(solution)/shard_map/ppermute | solution.py:551
  17.7 9.0 %collective-permute-start.8 = (bf16[1,7,24,768]{3,2,1,0:T(8,128)(2,1)S(1)}, bf16[1,7,24,768]{3,2,1,0:T(8,128)(2,1)S(1)}, u32[]{:S(2)}, u32[]{:S(2)}) collective-permute-start(bf16[1,7,24,768]{3,2,1,0:T(8,128)(2,1)S(1)} %maximum_bitcast_fusion.1), channel_id=1, source_target_pairs={{0,8},{1,17},{2,10},{3,19},{4,12},{5,21},{6,14},{7,23},{8,0},{9,25... | collective-permute-start | bytes 774152 | tf_op jit(solution)/shard_map/ppermute | solution.py:556
  18.4 8.4 %collective-permute-start.7 = (bf16[1,2,24,768]{3,2,1,0:T(8,128)(2,1)S(1)}, bf16[1,2,24,768]{3,2,1,0:T(8,128)(2,1)S(1)}, u32[]{:S(2)}, u32[]{:S(2)}) collective-permute-start(bf16[1,2,24,768]{3,2,1,0:T(8,128)(2,1)S(1)} %collective-permute-done.3), channel_id=1, source_target_pairs={{0,4},{1,3},{2,6},{3,1},{4,0},{5,7},{6,2},{7,5},{8,12},{9,11},{10,... | collective-permute-start | bytes 221192 | tf_op jit(solution)/shard_map/ppermute | solution.py:551
  26.9 15.6 %collective-permute-start.11 = (bf16[2,7,24,768]{3,2,1,0:T(8,128)(2,1)S(1)}, bf16[2,7,24,768]{3,2,1,0:T(8,128)(2,1)S(1)}, u32[]{:S(2)}, u32[]{:S(2)}) collective-permute-start(bf16[2,7,24,768]{3,2,1,0:T(8,128)(2,1)S(1)} %constant_dynamic-update-slice_fusion), channel_id=1, source_target_pairs={{0,16},{1,9},{2,18},{3,11},{4,20},{5,13},{6,22},{7,15},{8,24},{9,1... | collective-permute-start | bytes 1548296 | tf_op jit(solution)/shard_map/ppermute | solution.py:556
  27.5 7.7 %collective-permute-start.9 = (bf16[21,24,384]{2,1,0:T(8,128)(2,1)S(1)}, bf16[21,24,384]{2,1,0:T(8,128)(2,1)S(1)}, u32[]{:S(2)}, u32[]{:S(2)}) collective-permute-start(bf16[21,24,384]{2,1,0:T(8,128)(2,1)S(1)} %collective-permute-done.5.refs_2_), channel_id=1, source_target_pairs={{0,4},{1,3},{2,6},{3,1},{4,0},{5,7},{6,2},{7,5},{8,12},{9,11},{10,... | collective-permute-start | bytes 1161224 | tf_op jit(solution)/shard_map/ppermute | solution.py:551
  44.1 18.7 %collective-permute-start.14 = (bf16[4,7,24,768]{3,2,1,0:T(8,128)(2,1)}, bf16[4,7,24,768]{3,2,1,0:T(8,128)(2,1)}, u32[]{:S(2)}, u32[]{:S(2)}) collective-permute-start(bf16[4,7,24,768]{3,2,1,0:T(8,128)(2,1)} %constant_dynamic-update-slice_fusion.2.refs_1_), channel_id=1, source_target_pairs={{0,4},{1,3},{2,6},{3,1},{4,0},{5,7},{6,2},{7,5},{8,12},{9,11},{10,... | collective-permute-start | bytes 3096584 | tf_op jit(solution)/shard_map/ppermute | solution.py:551
  45.6 17.2 %collective-permute-start.13 = (bf16[4,7,24,768]{3,2,1,0:T(8,128)(2,1)}, bf16[4,7,24,768]{3,2,1,0:T(8,128)(2,1)}, u32[]{:S(2)}, u32[]{:S(2)}) collective-permute-start(bf16[4,7,24,768]{3,2,1,0:T(8,128)(2,1)} %constant_dynamic-update-slice_fusion.2.refs_1_), channel_id=1, source_target_pairs={{0,2},{1,5},{2,0},{3,7},{4,6},{5,1},{6,4},{7,3},{8,10},{9,13},{10,... | collective-permute-start | bytes 3096584 | tf_op jit(solution)/shard_map/ppermute | solution.py:551
  46.7 2.3 collective-permute-start.17
  47.9 12.6 %collective-permute-start.12 = (bf16[1,4,2,24,768]{4,3,2,1,0:T(8,128)(2,1)S(1)}, bf16[1,4,2,24,768]{4,3,2,1,0:T(8,128)(2,1)}, u32[]{:S(2)}, u32[]{:S(2)}) collective-permute-start(bf16[1,4,2,24,768]{4,3,2,1,0:T(8,128)(2,1)S(1)} %maximum_bitcast_fusion), channel_id=1, source_target_pairs={{0,8},{1,17},{2,10},{3,19},{4,12},{5,21},{6,14},{7,23},{8,0},{9,25... | collective-permute-start | bytes 884744 | tf_op jit(solution)/shard_map/ppermute | solution.py:556
  62.8 20.5 %collective-permute-start.19 = (bf16[4,7,24,768]{3,2,1,0:T(8,128)(2,1)}, bf16[4,7,24,768]{3,2,1,0:T(8,128)(2,1)S(1)}, u32[]{:S(2)}, u32[]{:S(2)}) collective-permute-start(bf16[4,7,24,768]{3,2,1,0:T(8,128)(2,1)} %constant_dynamic-update-slice_fusion.2.refs_1_), channel_id=1, source_target_pairs={{0,1},{1,0},{2,3},{3,2},{4,5},{5,4},{6,7},{7,6},{8,9},{9,8},{10,11... | collective-permute-start | bytes 3096584 | tf_op jit(solution)/shard_map/ppermute | solution.py:564
  62.8 20.6 %collective-permute-start.21 = (bf16[4,7,24,768]{3,2,1,0:T(8,128)(2,1)}, bf16[4,7,24,768]{3,2,1,0:T(8,128)(2,1)S(1)}, u32[]{:S(2)}, u32[]{:S(2)}) collective-permute-start(bf16[4,7,24,768]{3,2,1,0:T(8,128)(2,1)} %collective-permute-done.14.refs_3_), channel_id=1, source_target_pairs={{0,1},{1,0},{2,3},{3,2},{4,5},{5,4},{6,7},{7,6},{8,9},{9,8},{10,11... | collective-permute-start | bytes 3096584 | tf_op jit(solution)/shard_map/ppermute | solution.py:564
  63.3 20.1 %collective-permute-start.20 = (bf16[4,7,24,768]{3,2,1,0:T(8,128)(2,1)}, bf16[4,7,24,768]{3,2,1,0:T(8,128)(2,1)S(1)}, u32[]{:S(2)}, u32[]{:S(2)}) collective-permute-start(bf16[4,7,24,768]{3,2,1,0:T(8,128)(2,1)} %collective-permute-done.13.refs_2_), channel_id=1, source_target_pairs={{0,1},{1,0},{2,3},{3,2},{4,5},{5,4},{6,7},{7,6},{8,9},{9,8},{10,11... | collective-permute-start | bytes 3096584 | tf_op jit(solution)/shard_map/ppermute | solution.py:564
  63.3 20.1 %collective-permute-start.18 = (bf16[4,7,24,768]{3,2,1,0:T(8,128)(2,1)}, bf16[4,7,24,768]{3,2,1,0:T(8,128)(2,1)}, u32[]{:S(2)}, u32[]{:S(2)}) collective-permute-start(bf16[4,7,24,768]{3,2,1,0:T(8,128)(2,1)} %collective-permute-done.13.refs_2_), channel_id=1, source_target_pairs={{0,4},{1,3},{2,6},{3,1},{4,0},{5,7},{6,2},{7,5},{8,12},{9,11},{10,... | collective-permute-start | bytes 3096584 | tf_op jit(solution)/shard_map/ppermute | solution.py:551
  66.0 17.3 %collective-permute-start.22 = (bf16[2,4,2,24,768]{4,3,2,1,0:T(8,128)(2,1)S(1)}, bf16[2,4,2,24,768]{4,3,2,1,0:T(8,128)(2,1)}, u32[]{:S(2)}, u32[]{:S(2)}) collective-permute-start(bf16[2,4,2,24,768]{4,3,2,1,0:T(8,128)(2,1)S(1)} %constant_dynamic-update-slice_fusion.4.refs_9_), channel_id=1, source_target_pairs={{0,16},{1,9},{2,18},{3,11},{4,20},{5,13},{6,22},{7,15},{8,24},{9,1... | collective-permute-start | bytes 1769480 | tf_op jit(solution)/shard_map/ppermute | solution.py:556
  83.4 5.7 %collective-permute-start.23 = (bf16[4,7,24,768]{3,2,1,0:T(8,128)(2,1)}, bf16[4,7,24,768]{3,2,1,0:T(8,128)(2,1)}, u32[]{:S(2)}, u32[]{:S(2)}) collective-permute-start(bf16[4,7,24,768]{3,2,1,0:T(8,128)(2,1)} %collective-permute-done.18.refs_4_), channel_id=1, source_target_pairs={{0,1},{1,0},{2,3},{3,2},{4,5},{5,4},{6,7},{7,6},{8,9},{9,8},{10,11... | collective-permute-start | bytes 3096584 | tf_op jit(solution)/shard_map/ppermute | solution.py:564
  83.5 3.9 %collective-permute-start.24 = (bf16[2,4,2,24,768]{4,3,2,1,0:T(8,128)(2,1)S(1)}, bf16[2,4,2,24,768]{4,3,2,1,0:T(8,128)(2,1)S(1)}, u32[]{:S(2)}, u32[]{:S(2)}) collective-permute-start(bf16[2,4,2,24,768]{4,3,2,1,0:T(8,128)(2,1)S(1)} %constant_dynamic-update-slice_fusion.4.refs_9_), channel_id=1, source_target_pairs={{0,1},{1,0},{2,3},{3,2},{4,5},{5,4},{6,7},{7,6},{8,9},{9,8},{10,11... | collective-permute-start | bytes 1769480 | tf_op jit(solution)/shard_map/ppermute | solution.py:564
  84.0 4.3 %collective-permute-start.25 = (bf16[2,4,2,24,768]{4,3,2,1,0:T(8,128)(2,1)}, bf16[2,4,2,24,768]{4,3,2,1,0:T(8,128)(2,1)S(1)}, u32[]{:S(2)}, u32[]{:S(2)}) collective-permute-start(bf16[2,4,2,24,768]{4,3,2,1,0:T(8,128)(2,1)} %collective-permute-done.22.refs_10_), channel_id=1, source_target_pairs={{0,1},{1,0},{2,3},{3,2},{4,5},{5,4},{6,7},{7,6},{8,9},{9,8},{10,11... | collective-permute-start | bytes 1769480 | tf_op jit(solution)/shard_map/ppermute | solution.py:564
  137.8 10.8 %collective-permute-start.26 = (bf16[8,5,24,768]{3,2,1,0:T(8,128)(2,1)}, bf16[8,5,24,768]{3,2,1,0:T(8,128)(2,1)S(1)}, u32[]{:S(2)}, u32[]{:S(2)}) collective-permute-start(bf16[8,5,24,768]{3,2,1,0:T(8,128)(2,1)} %bitcast.61), channel_id=1, source_target_pairs={{0,1},{1,0},{2,3},{3,2},{4,5},{5,4},{6,7},{7,6},{8,9},{9,8},{10,11... | collective-permute-start | bytes 4423688 | tf_op jit(solution)/shard_map/ppermute | solution.py:564
  138.2 10.5 %collective-permute-start.27 = (bf16[8,5,24,768]{3,2,1,0:T(8,128)(2,1)}, bf16[8,5,24,768]{3,2,1,0:T(8,128)(2,1)S(1)}, u32[]{:S(2)}, u32[]{:S(2)}) collective-permute-start(bf16[8,5,24,768]{3,2,1,0:T(8,128)(2,1)} %bitcast.60), channel_id=1, source_target_pairs={{0,1},{1,0},{2,3},{3,2},{4,5},{5,4},{6,7},{7,6},{8,9},{9,8},{10,11... | collective-permute-start | bytes 4423688 | tf_op jit(solution)/shard_map/ppermute | solution.py:564
  148.3 5.7 %collective-permute-start.28 = (bf16[8,4,24,768]{3,2,1,0:T(8,128)(2,1)}, bf16[8,4,24,768]{3,2,1,0:T(8,128)(2,1)S(1)}, u32[]{:S(2)}, u32[]{:S(2)}) collective-permute-start(bf16[8,4,24,768]{3,2,1,0:T(8,128)(2,1)} %get-tuple-element.170), channel_id=1, source_target_pairs={{0,1},{1,0},{2,3},{3,2},{4,5},{5,4},{6,7},{7,6},{8,9},{9,8},{10,11... | collective-permute-start | bytes 3538952 | tf_op jit(solution)/shard_map/ppermute | solution.py:564
  152.2 37.0 %collective-permute-start.31 = (bf16[8,5,24,768]{3,2,1,0:T(8,128)(2,1)S(1)}, bf16[8,5,24,768]{3,2,1,0:T(8,128)(2,1)}, u32[]{:S(2)}, u32[]{:S(2)}) collective-permute-start(bf16[8,5,24,768]{3,2,1,0:T(8,128)(2,1)S(1)} %fusion.refs_8_), channel_id=1, source_target_pairs={{0,2},{1,5},{2,0},{3,7},{4,6},{5,1},{6,4},{7,3},{8,10},{9,13},{10,... | collective-permute-start | bytes 4423688 | tf_op jit(solution)/shard_map/ppermute | solution.py:551
  154.4 34.9 %collective-permute-start.32 = (bf16[8,4,24,768]{3,2,1,0:T(8,128)(2,1)S(1)}, bf16[8,4,24,768]{3,2,1,0:T(8,128)(2,1)}, u32[]{:S(2)}, u32[]{:S(2)}) collective-permute-start(bf16[8,4,24,768]{3,2,1,0:T(8,128)(2,1)S(1)} %add_convert_fusion.refs_9_), channel_id=1, source_target_pairs={{0,8},{1,17},{2,10},{3,19},{4,12},{5,21},{6,14},{7,23},{8,0},{9,25... | collective-permute-start | bytes 3538952 | tf_op jit(solution)/shard_map/ppermute | solution.py:556
  154.4 34.8 %collective-permute-start.33 = (bf16[8,4,24,768]{3,2,1,0:T(8,128)(2,1)}, bf16[8,4,24,768]{3,2,1,0:T(8,128)(2,1)}, u32[]{:S(2)}, u32[]{:S(2)}) collective-permute-start(bf16[8,4,24,768]{3,2,1,0:T(8,128)(2,1)} %get-tuple-element.190), channel_id=1, source_target_pairs={{0,1},{1,0},{2,3},{3,2},{4,5},{5,4},{6,7},{7,6},{8,9},{9,8},{10,11... | collective-permute-start | bytes 3538952 | tf_op jit(solution)/shard_map/ppermute | solution.py:564
  188.7 4.1 %collective-permute-start.29 = (bf16[8,5,24,384]{3,2,1,0:T(8,128)(2,1)}, bf16[8,5,24,384]{3,2,1,0:T(8,128)(2,1)S(1)}, u32[]{:S(2)}, u32[]{:S(2)}) collective-permute-start(bf16[8,5,24,384]{3,2,1,0:T(8,128)(2,1)} %get-tuple-element.184), channel_id=1, source_target_pairs={{0,1},{1,0},{2,3},{3,2},{4,5},{5,4},{6,7},{7,6},{8,9},{9,8},{10,11... | collective-permute-start | bytes 2211848 | tf_op jit(solution)/shard_map/ppermute | solution.py:564
  188.7 4.0 %collective-permute-start.30 = (bf16[8,5,24,384]{3,2,1,0:T(8,128)(2,1)}, bf16[8,5,24,384]{3,2,1,0:T(8,128)(2,1)S(1)}, u32[]{:S(2)}, u32[]{:S(2)}) collective-permute-start(bf16[8,5,24,384]{3,2,1,0:T(8,128)(2,1)} %get-tuple-element.185), channel_id=1, source_target_pairs={{0,1},{1,0},{2,3},{3,2},{4,5},{5,4},{6,7},{7,6},{8,9},{9,8},{10,11... | collective-permute-start | bytes 2211848 | tf_op jit(solution)/shard_map/ppermute | solution.py:564
  193.0 18.7 %collective-permute-start.34 = (bf16[8,5,24,384]{3,2,1,0:T(8,128)(2,1)S(1)}, bf16[8,5,24,384]{3,2,1,0:T(8,128)(2,1)}, u32[]{:S(2)}, u32[]{:S(2)}) collective-permute-start(bf16[8,5,24,384]{3,2,1,0:T(8,128)(2,1)S(1)} %add_convert_fusion.1.refs_14_), channel_id=1, source_target_pairs={{0,2},{1,5},{2,0},{3,7},{4,6},{5,1},{6,4},{7,3},{8,10},{9,13},{10,... | collective-permute-start | bytes 2211848 | tf_op jit(solution)/shard_map/ppermute | solution.py:551
  193.8 17.9 %collective-permute-start.35 = (bf16[4,5,24,768]{3,2,1,0:T(8,128)(2,1)S(1)}, bf16[4,5,24,768]{3,2,1,0:T(8,128)(2,1)}, u32[]{:S(2)}, u32[]{:S(2)}) collective-permute-start(bf16[4,5,24,768]{3,2,1,0:T(8,128)(2,1)S(1)} %fusion.2.refs_15_), channel_id=1, source_target_pairs={{0,4},{1,3},{2,6},{3,1},{4,0},{5,7},{6,2},{7,5},{8,12},{9,11},{10,... | collective-permute-start | bytes 2211848 | tf_op jit(solution)/shard_map/ppermute | solution.py:551
  194.5 17.1 %collective-permute-start.36 = (bf16[4,4,24,768]{3,2,1,0:T(8,128)(2,1)S(1)}, bf16[4,4,24,768]{3,2,1,0:T(8,128)(2,1)S(1)}, u32[]{:S(2)}, u32[]{:S(2)}) collective-permute-start(bf16[4,4,24,768]{3,2,1,0:T(8,128)(2,1)S(1)} %add_convert_fusion.2.refs_16_), channel_id=1, source_target_pairs={{0,16},{1,9},{2,18},{3,11},{4,20},{5,13},{6,22},{7,15},{8,24},{9,1... | collective-permute-start | bytes 1769480 | tf_op jit(solution)/shard_map/ppermute | solution.py:556
  213.2 16.4 %collective-permute-start.37 = (bf16[4,5,24,384]{3,2,1,0:T(8,128)(2,1)S(1)}, bf16[4,5,24,384]{3,2,1,0:T(8,128)(2,1)}, u32[]{:S(2)}, u32[]{:S(2)}) collective-permute-start(bf16[4,5,24,384]{3,2,1,0:T(8,128)(2,1)S(1)} %add_convert_fusion.4.refs_5_), channel_id=1, source_target_pairs={{0,4},{1,3},{2,6},{3,1},{4,0},{5,7},{6,2},{7,5},{8,12},{9,11},{10,... | collective-permute-start | bytes 1105928 | tf_op jit(solution)/shard_map/ppermute | solution.py:551
  216.0 13.6 %collective-permute-start.38 = (bf16[2,5,24,768]{3,2,1,0:T(8,128)(2,1)S(1)}, bf16[2,5,24,768]{3,2,1,0:T(8,128)(2,1)}, u32[]{:S(2)}, u32[]{:S(2)}) collective-permute-start(bf16[2,5,24,768]{3,2,1,0:T(8,128)(2,1)S(1)} %add_convert_fusion.3.refs_6_), channel_id=1, source_target_pairs={{0,8},{1,17},{2,10},{3,19},{4,12},{5,21},{6,14},{7,23},{8,0},{9,25... | collective-permute-start | bytes 1105928 | tf_op jit(solution)/shard_map/ppermute | solution.py:556
  217.7 11.9 %collective-permute-start.39 = (bf16[2,4,24,768]{3,2,1,0:T(8,128)(2,1)S(1)}, bf16[2,4,24,768]{3,2,1,0:T(8,128)(2,1)S(1)}, u32[]{:S(2)}, u32[]{:S(2)}) collective-permute-start(bf16[2,4,24,768]{3,2,1,0:T(8,128)(2,1)S(1)} %add_convert_fusion.5.refs_7_), channel_id=1, source_target_pairs={{0,2},{1,5},{2,0},{3,7},{4,6},{5,1},{6,4},{7,3},{8,10},{9,13},{10,... | collective-permute-start | bytes 884744 | tf_op jit(solution)/shard_map/ppermute | solution.py:551
  219.1 10.5 %collective-permute-start.40 = (f32[4,1104]{1,0:T(4,128)}, f32[4,1104]{1,0:T(4,128)S(1)}, u32[]{:S(2)}, u32[]{:S(2)}) collective-permute-start(f32[4,1104]{1,0:T(4,128)} %get-tuple-element.205), channel_id=1, source_target_pairs={{0,1},{1,0},{2,3},{3,2},{4,5},{5,4},{6,7},{7,6},{8,9},{9,8},{10,11... | collective-permute-start | bytes 53000 | tf_op jit(solution)/shard_map/ppermute | solution.py:564
  230.9 8.6 %collective-permute-start.44 = (bf16[2,5,24,384]{3,2,1,0:T(8,128)(2,1)S(1)}, bf16[2,5,24,384]{3,2,1,0:T(8,128)(2,1)S(1)}, u32[]{:S(2)}, u32[]{:S(2)}) collective-permute-start(bf16[2,5,24,384]{3,2,1,0:T(8,128)(2,1)S(1)} %add_convert_fusion.7), channel_id=1, source_target_pairs={{0,8},{1,17},{2,10},{3,19},{4,12},{5,21},{6,14},{7,23},{8,0},{9,25... | collective-permute-start | bytes 552968 | tf_op jit(solution)/shard_map/ppermute | solution.py:556
  232.7 9.8 %collective-permute-start.43 = (f32[1104]{0:T(1024)S(1)}, f32[1104]{0:T(1024)S(1)}, u32[]{:S(2)}, u32[]{:S(2)}) collective-permute-start(f32[1104]{0:T(1024)S(1)} %get-tuple-element.218), channel_id=1, source_target_pairs={{0,6},{1,7},{2,4},{3,5},{4,2},{5,3},{6,0},{7,1},{8,14},{9,15},{10,... | collective-permute-start | bytes 13256 | tf_op jit(solution)/shard_map/ppermute | solution.py:564
  233.6 8.8 %collective-permute-start.42 = (f32[1104]{0:T(1024)S(1)}, f32[1104]{0:T(1024)S(1)}, u32[]{:S(2)}, u32[]{:S(2)}) collective-permute-start(f32[1104]{0:T(1024)S(1)} %get-tuple-element.219), channel_id=1, source_target_pairs={{0,4},{1,5},{2,6},{3,7},{4,0},{5,1},{6,2},{7,3},{8,12},{9,13},{10,... | collective-permute-start | bytes 13256 | tf_op jit(solution)/shard_map/ppermute | solution.py:564
  234.9 7.5 %collective-permute-start.41 = (f32[1104]{0:T(1024)S(1)}, f32[1104]{0:T(1024)S(1)}, u32[]{:S(2)}, u32[]{:S(2)}) collective-permute-start(f32[1104]{0:T(1024)S(1)} %get-tuple-element.220), channel_id=1, source_target_pairs={{0,2},{1,3},{2,0},{3,1},{4,6},{5,7},{6,4},{7,5},{8,10},{9,11},{10,... | collective-permute-start | bytes 13256 | tf_op jit(solution)/shard_map/ppermute | solution.py:564
  237.4 9.5 %collective-permute-start.50 = (bf16[1,4,24,768]{3,2,1,0:T(8,128)(2,1)S(1)}, bf16[1,4,24,768]{3,2,1,0:T(8,128)(2,1)S(1)}, u32[]{:S(2)}, u32[]{:S(2)}) collective-permute-start(bf16[1,4,24,768]{3,2,1,0:T(8,128)(2,1)S(1)} %add_convert_fusion.8), channel_id=1, source_target_pairs={{0,4},{1,3},{2,6},{3,1},{4,0},{5,7},{6,2},{7,5},{8,12},{9,11},{10,... | collective-permute-start | bytes 442376 | tf_op jit(solution)/shard_map/ppermute | solution.py:551
  239.6 8.9 %collective-permute-start.49 = (bf16[1,5,24,768]{3,2,1,0:T(8,128)(2,1)S(1)}, bf16[1,5,24,768]{3,2,1,0:T(8,128)(2,1)S(1)}, u32[]{:S(2)}, u32[]{:S(2)}) collective-permute-start(bf16[1,5,24,768]{3,2,1,0:T(8,128)(2,1)S(1)} %add_convert_fusion.6), channel_id=1, source_target_pairs={{0,16},{1,9},{2,18},{3,11},{4,20},{5,13},{6,22},{7,15},{8,24},{9,1... | collective-permute-start | bytes 552968 | tf_op jit(solution)/shard_map/ppermute | solution.py:556
  242.5 11.4 %collective-permute-start.47 = (f32[1104]{0:T(1024)S(1)}, f32[1104]{0:T(1024)S(1)}, u32[]{:S(2)}, u32[]{:S(2)}) collective-permute-start(f32[1104]{0:T(1024)S(1)} %add_add_fusion.2), channel_id=1, source_target_pairs={{0,24},{8,16},{16,8},{24,0},{1,25},{9,17},{17,9},{25,1},{2,26},{10... | collective-permute-start | bytes 13256 | tf_op jit(solution)/shard_map/ppermute | solution.py:560
  244.0 9.8 %collective-permute-start.46 = (f32[1104]{0:T(1024)S(1)}, f32[1104]{0:T(1024)S(1)}, u32[]{:S(2)}, u32[]{:S(2)}) collective-permute-start(f32[1104]{0:T(1024)S(1)} %add_add_fusion.2), channel_id=1, source_target_pairs={{0,16},{8,24},{16,0},{24,8},{1,17},{9,25},{17,1},{25,9},{2,18},{10... | collective-permute-start | bytes 13256 | tf_op jit(solution)/shard_map/ppermute | solution.py:560
  244.3 9.5 %collective-permute-start.45 = (f32[1104]{0:T(1024)S(1)}, f32[1104]{0:T(1024)S(1)}, u32[]{:S(2)}, u32[]{:S(2)}) collective-permute-start(f32[1104]{0:T(1024)S(1)} %add_add_fusion.2), channel_id=1, source_target_pairs={{0,8},{8,0},{16,24},{24,16},{1,9},{9,1},{17,25},{25,17},{2,10},{10... | collective-permute-start | bytes 13256 | tf_op jit(solution)/shard_map/ppermute | solution.py:560
  251.9 5.5 %collective-permute-start.48 = (bf16[1,5,24,384]{3,2,1,0:T(8,128)(2,1)S(1)}, bf16[1,5,24,384]{3,2,1,0:T(8,128)(2,1)S(1)}, u32[]{:S(2)}, u32[]{:S(2)}) collective-permute-start(bf16[1,5,24,384]{3,2,1,0:T(8,128)(2,1)S(1)} %add_convert_fusion.9), channel_id=1, source_target_pairs={{0,16},{1,9},{2,18},{3,11},{4,20},{5,13},{6,22},{7,15},{8,24},{9,1... | collective-permute-start | bytes 276488 | tf_op jit(solution)/shard_map/ppermute | solution.py:556
  (38 other events, 252.8 us)
where the time goes:
time: 260 us; the launch traced here: 259 us
  Pallas kernels  136 us (52%)
  starting transfers between devices  44.6 us (17%)
  waiting for transfers between devices  41.7 us (16%)
  other arithmetic  22.5 us (9%)
  local copies, waits for them, and re-layouts  12.8 us (5%)
    pallas_call x11, Pallas kernels, call(): pl.pallas_call(body, grid_spec=pltpu.PrefetchScalarGridSpec(num_scalar_pr...  136 us
    ppermute x15, starting transfers between devices, plane_step(): lax.ppermute(v, 'fsdp', [(i, i ^ (2 if i % 2 == step else 4)) for i in ra...  18.9 us
    ppermute x10, waiting for transfers between devices, depth_step(): return lax.ppermute(v, AXES, pairs)  18.8 us
    ppermute x15, waiting for transfers between devices, plane_step(): lax.ppermute(v, 'fsdp', [(i, i ^ (2 if i % 2 == step else 4)) for i in ra...  16.4 us
    convert_element_type x9, other arithmetic, upper(): return sum((t[n // 2:n].astype(F32) for t in self.terms)).astype(BF)  12.5 us
    ppermute x6, starting transfers between devices, depth_swap(): return lax.ppermute(v, 'dp', [(i, i ^ bits) for i in range(4)])  10.2 us
    ppermute x10, starting transfers between devices, depth_step(): return lax.ppermute(v, AXES, pairs)  8.53 us
    ppermute x20, starting transfers between devices, fsdp_swap(): return lax.ppermute(v, 'fsdp', [(i, i ^ bit) for i in range(8)])  6.94 us
  transfers between devices with their start and end apart: 51, of which 16 were waited for; matrix products, arithmetic and copies ran while one was open for 9% of the time, Pallas kernels for 34%

commit v1 on v0

--- a/solution.py
+++ b/solution.py
@@ -472,7 +472,7 @@
         into=into,
         scratch_shapes=[pltpu.VMEM((rows, d), F32)],
         waits=waits,
-        vmem=VMEM,
+        vmem=48,
         cost=8,
         name="output",
     )
@@ -529,7 +529,7 @@
         out_shape=[shape_of((rows, d))] + [shape_of(t, F32) for t in vecs],
         scratch_shapes=[pltpu.VMEM((1, n), F32)],
         waits=waits,
-        vmem=VMEM,
+        vmem=48,
         cost=9,
         name="input_grad",
     )
@@ -665,8 +665,39 @@
         n = got.shape[0]
         return sum(t[n // 2 : n].astype(F32) for t in self.terms).astype(BF)
 
-    def total(self, got, part):
-        return sum(t[0, part].astype(F32) for t in self.terms + [got])
+    def last(self, got):
+        return self.terms + [got]
+
+
+def totals(chain, groups, shapes, name):
+    def kernel(*refs):
+        outs = list(refs[sum(len(g) for g in groups) :])
+        at = 0
+        for g, results in zip(groups, shapes):
+            terms = refs[at : at + len(g)]
+            at += len(g)
+            rows, n = g[0].shape[2:]
+            q = 0
+            for shape in results:
+                out = outs.pop(0)
+                for r in range(0, shape[0], rows):
+                    for c in range(0, shape[1], n):
+                        out[r : r + rows, c : c + n] = sum(t[0, q].astype(F32) for t in terms)
+                        q += 1
+
+    flat = [t for g in groups for t in g]
+    made = [shape_of(s, F32) for results in shapes for s in results]
+    return chain.call(
+        kernel,
+        flat,
+        grid=(1,),
+        in_specs=[pl.BlockSpec((1, *t.shape[1:]), lambda i: (0, 0, 0, 0)) for t in flat],
+        out_specs=[resident(t) for t in made],
+        out_shape=made,
+        vmem=24,
+        cost=3,
+        name=name,
+    )
 
 
 def hand_out(where_ref, acc, piece, own, sib, depth_first):
@@ -932,10 +963,14 @@
     got_d, got_u = after((got_d, got_u), send_q)
     v = v[0] + sum(got_vec)
     grad_vectors = v + sum(depth_swap(v, bits) for bits in (1, 2, 3))
-    grad_down, grad_out = sum_d.total(got_d, slice(0, tall)).reshape(tall * piece, d), sum_d.total(got_d, tall)
-    wide = lambda t: t.transpose(1, 0, 2).reshape(piece, -1)
-    grad_up = wide(sum_u.total(got_u, slice(None)))
-    grad_qkv = wide(sum_q.total(got_q, slice(None)))
+    grad_down, grad_out, grad_up = totals(
+        chain,
+        [sum_d.last(got_d), sum_u.last(got_u)],
+        [[(tall * piece, d), (piece, d)], [(piece, tall * d)]],
+        "feed_sums",
+    )
+    got_q = after(got_q, grad_up)
+    grad_qkv, = totals(chain, [sum_q.last(got_q)], [[(piece, w_qkv.shape[1])]], "qkv_sum")
     return output, grad_tokens, dfirst, grad_vectors, grad_qkv, grad_out, grad_up, grad_down
 
 

time: 260 us -> 246 us (0.946)
  other arithmetic: 22.5 us -> 10.7 us
  local copies, waits for them, and re-layouts: 12.8 us -> 9.2 us
    convert_element_type x9, other arithmetic: 12.5 us -> 4.67 us  [upper(): return sum((t[n // 2:n].astype(F32) for t in self.terms)).astype(BF)]
    add x2 -> x0, other arithmetic: 3.43 us -> none  [total(): return sum((t[0, part].astype(F32) for t in self.terms + [got]))]
    unnamed x73 -> x75, local copies, waits for them, and re-layouts: 6.92 us -> 4.78 us
    pallas_call x11 -> x13, Pallas kernels: 136 us -> 137 us  [call(): pl.pallas_call(body, grid_spec=pltpu.PrefetchScalarGridSpec(num_scalar_pr...]
  transfers between devices with their start and end apart: 51 -> 51, of which waited for: 16 -> 17; matrix products, arithmetic and copies ran while one was open for 9% -> 6% of each run, Pallas kernels for 34% -> 36%
where the time goes in v1:
time: 246 us; the launch traced here: 245 us
  Pallas kernels  137 us (56%)
  starting transfers between devices  45.1 us (18%)
  waiting for transfers between devices  42 us (17%)
  other arithmetic  10.7 us (4%)
  local copies, waits for them, and re-layouts  9.2 us (4%)
    pallas_call x13, Pallas kernels, call(): pl.pallas_call(body, grid_spec=pltpu.PrefetchScalarGridSpec(num_scalar_pr...  137 us
    ppermute x15, starting transfers between devices, plane_step(): lax.ppermute(v, 'fsdp', [(i, i ^ (2 if i % 2 == step else 4)) for i in ra...  18.5 us
    ppermute x10, waiting for transfers between devices, depth_step(): return lax.ppermute(v, AXES, pairs)  18.1 us
    ppermute x15, waiting for transfers between devices, plane_step(): lax.ppermute(v, 'fsdp', [(i, i ^ (2 if i % 2 == step else 4)) for i in ra...  16.3 us
    ppermute x6, starting transfers between devices, depth_swap(): return lax.ppermute(v, 'dp', [(i, i ^ bits) for i in range(4)])  10.2 us
    ppermute x10, starting transfers between devices, depth_step(): return lax.ppermute(v, AXES, pairs)  9.57 us
    ppermute x20, waiting for transfers between devices, fsdp_swap(): return lax.ppermute(v, 'fsdp', [(i, i ^ bit) for i in range(8)])  7.27 us
    ppermute x20, starting transfers between devices, fsdp_swap(): return lax.ppermute(v, 'fsdp', [(i, i ^ bit) for i in range(8)])  6.82 us
  transfers between devices with their start and end apart: 51, of which 17 were waited for; matrix products, arithmetic and copies ran while one was open for 6% of the time, Pallas kernels for 36%

profile of v1, /device:TPU:0, one launch (start us, length us, event | category | flops | bytes accessed | tf_op | source)
XLA Modules:
  0.0 245.5 jit_solution(17452410103759525545)
XLA Ops:
  0.6 5.1 %collective-permute-start.2 = (bf16[1,24,1920]{2,1,0:T(8,128)(2,1)}, bf16[1,24,1920]{2,1,0:T(8,128)(2,1)S(1)}, u32[]{:S(2)}, u32[]{:S(2)}) collective-permute-start(bf16[1,24,1920]{2,1,0:T(8,128)(2,1)} %bitcast.30), channel_id=1, source_target_pairs={{0,24},{8,16},{16,8},{24,0},{1,25},{9,17},{17,9},{25,1},{2,26},{10... | collective-permute-start | bytes 276488 | tf_op jit(solution)/shard_map/ppermute | solution.py:560
  6.4 0.9 fusion.3
  7.3 1.7 collective-permute-start.4
  9.1 1.5 collective-permute-start.3
  11.2 0.9 copy.20
  14.7 1.6 collective-permute-start.6
  16.3 1.5 collective-permute-start.5
  19.2 7.6 %collective-permute-done.7 = bf16[1,2,24,768]{3,2,1,0:T(8,128)(2,1)S(1)} collective-permute-done((bf16[1,2,24,768]{3,2,1,0:T(8,128)(2,1)S(1)}, bf16[1,2,24,768]{3,2,1,0:T(8,128)(2,1)S(1)}, u32[]{:S(2)}, u32[]{:S(2)}) %collective-permute-start.7) | collective-permute-done | bytes 73760 | tf_op jit(solution)/shard_map/ppermute | solution.py:551
  27.5 1.1 collective-permute-start.9
  29.2 6.0 %collective-permute-done.9.refs_4_ = bf16[21,24,384]{2,1,0:T(8,128)(2,1)S(1)} collective-permute-done((bf16[21,24,384]{2,1,0:T(8,128)(2,1)S(1)}, bf16[21,24,384]{2,1,0:T(8,128)(2,1)S(1)}, u32[]{:S(2)}, u32[]{:S(2)}) %collective-permute-start.9) | collective-permute-done | bytes 387104 | tf_op jit(solution)/shard_map/ppermute | solution.py:551
  35.2 7.2 %collective-permute-done.11 = bf16[2,7,24,768]{3,2,1,0:T(8,128)(2,1)S(1)} collective-permute-done((bf16[2,7,24,768]{3,2,1,0:T(8,128)(2,1)S(1)}, bf16[2,7,24,768]{3,2,1,0:T(8,128)(2,1)S(1)}, u32[]{:S(2)}, u32[]{:S(2)}) %collective-permute-start.11) | collective-permute-done | bytes 516128 | tf_op jit(solution)/shard_map/ppermute | solution.py:556
  44.1 1.5 collective-permute-start.14
  46.7 1.2 collective-permute-done.16.refs_7_
  50.9 9.5 %project.1 = (bf16[1024,768]{1,0:T(8,128)(2,1)}, bf16[1024,768]{1,0:T(8,128)(2,1)}, bf16[1024,768]{1,0:T(8,128)(2,1)}, bf16[1024,768]{1,0:T(8,128)(2,1)}, bf16[768,1920]{1,0:T(8,128)(2,1)}, /*index=5*/f32[8,128]{1,0:T(8,128)}) custom-call(s32[3]{0:T(128)} %copy-done.18, bf16[21,24,384]{2,1,0:T(8,128)(2,1)} %copy-done.7, bf16[21,24,384]{2,1,0:T(8,128)(2,1)} %copy-done.9, ...), custom_call_target="tpu_custom_call" | custom-call | flops 92000000 | bytes 295200 | tf_op jit(solution)/shard_map/project/pallas_call | solution.py:80
  60.5 2.3 collective-permute-done.14.refs_3_
  63.3 1.7 collective-permute-start.18
  65.1 1.0 constant_dynamic-update-slice_fusion.4.refs_9_
  66.1 1.3 collective-permute-start.22
  67.3 13.8 %attend_forward.1 = (bf16[1024,768]{1,0:T(8,128)(2,1)}, f32[6,2,1024]{2,1,0:T(2,128)}, f32[8,128]{1,0:T(8,128)}) custom-call(s32[1,2]{1,0:T(1,128)} %refs_0_.3, bf16[1024,768]{1,0:T(8,128)(2,1)} %get-tuple-element.149.refs_1_, bf16[1024,768]{1,0:T(8,128)(2,1)} %get-tuple-element.150.refs_2_, bf16[1024,768]{1,0:T(8,128)(2,1)} %get-tuple-element.151.refs_3_, ...), custom_call_target="tpu_custom_call" | custom-call | flops 241500000 | bytes 774900 | tf_op jit(solution)/shard_map/attend_forward/pallas_call | solution.py:80
  81.2 2.2 collective-permute-done.22.refs_10_
  84.1 3.4 %collective-permute-done.24.refs_11_ = bf16[2,4,2,24,768]{4,3,2,1,0:T(8,128)(2,1)S(1)} collective-permute-done((bf16[2,4,2,24,768]{4,3,2,1,0:T(8,128)(2,1)S(1)}, bf16[2,4,2,24,768]{4,3,2,1,0:T(8,128)(2,1)S(1)}, u32[]{:S(2)}, u32[]{:S(2)}) %collective-permute-start.24) | collective-permute-done | bytes 589856 | tf_op jit(solution)/shard_map/ppermute | solution.py:564
  89.1 35.5 %feed_forward.1 = (f32[1024,768]{1,0:T(8,128)}, bf16[1024,768]{1,0:T(8,128)(2,1)}, bf16[1024,3072]{1,0:T(8,128)(2,1)}, bf16[1024,3072]{1,0:T(8,128)(2,1)}, f32[1...) custom-call(s32[3]{0:T(128)} %copy-done.18, ...), custom_call_target="tpu_custom_call" | custom-call | flops 356500000 | bytes 1143900 | tf_op jit(solution)/shard_map/feed_forward/pallas_call | solution.py:80
  124.6 13.2 %down_out_grad.1 = (bf16[2,4,5,24,768]{4,3,2,1,0:T(8,128)(2,1)}, bf16[2,4,5,24,768]{4,3,2,1,0:T(8,128)(2,1)}, bf16[2,4,5,24,768]{4,3,2,1,0:T(8,128)(2,1)}, bf16[2,4,5,24,768]{4,3,2,1,0:T(8,128)(2,1)}, f32[8,128]{1,0:T(8,128)}) custom-call(s32[3]{0:T(128)} %copy-done.18, bf16[1024,3072]{1,0:T(8,128)(2,1)} %get-tuple-element.160.refs_1_.refs_0_, ...), custom_call_target="tpu_custom_call" | custom-call | flops 143750000 | bytes 461250 | tf_op jit(solution)/shard_map/down_out_grad/pallas_call | solution.py:80
  138.4 10.0 %up_grad.1 = (bf16[8,4,24,768]{3,2,1,0:T(8,128)(2,1)}, bf16[8,4,24,768]{3,2,1,0:T(8,128)(2,1)}, bf16[8,4,24,768]{3,2,1,0:T(8,128)(2,1)}, bf16[8,4,24,768]{3,2,1,0:T(8,128)(2,1)}, f32[8,128]{1,0:T(8,128)}) custom-call(s32[3]{0:T(128)} %copy-done.18, bf16[1024,768]{1,0:T(8,128)(2,1)} %get-tuple-element.165.refs_1_, ...), custom_call_target="tpu_custom_call" | custom-call | flops 103500000 | bytes 332100 | tf_op jit(solution)/shard_map/up_grad/pallas_call | solution.py:80
  148.8 2.9 %fusion.refs_8_ = bf16[8,5,24,768]{3,2,1,0:T(8,128)(2,1)} fusion(bf16[8,5,24,768]{3,2,1,0:T(8,128)(2,1)} %collective-permute-done.27, bf16[2,4,5,24,768]{4,3,2,1,0:T(8,128)(2,1)S(1)} %copy-done.27), kind=kLoop, calls=%fused_computation.1 | loop fusion | flops 2949120 | bytes 4423680 | tf_op jit(solution)/shard_map/convert_element_type | solution.py:661
  151.8 1.7 collective-permute-start.31
  153.5 1.3 add_convert_fusion.refs_9_
  154.9 23.7 %attend_backward.1 = (bf16[1024,768]{1,0:T(8,128)(2,1)}, bf16[1024,768]{1,0:T(8,128)(2,1)}, bf16[1024,384]{1,0:T(8,128)(2,1)}, bf16[1024,384]{1,0:T(8,128)(2,1)}, f32[8,128]{1,0:T(8,128)}) custom-call(s32[1,2]{1,0:T(1,128)} %refs_0_.3, bf16[1024,768]{1,0:T(8,128)(2,1)} %get-tuple-element.149.refs_1_, bf16[1024,768]{1,0:T(8,128)(2,1)} %get-tuple-element.150.refs_2_, ...), custom_call_target="tpu_custom_call" | custom-call | flops 414000000 | bytes 1328400 | tf_op jit(solution)/shard_map/attend_backward/pallas_call | solution.py:80
  178.5 9.6 %qkv_grad.1 = (bf16[8,5,24,384]{3,2,1,0:T(8,128)(2,1)}, bf16[8,5,24,384]{3,2,1,0:T(8,128)(2,1)}, bf16[8,5,24,384]{3,2,1,0:T(8,128)(2,1)}, bf16[8,5,24,384]{3,2,1,0:T(8,128)(2,1)}, f32[8,128]{1,0:T(8,128)}) custom-call(s32[3]{0:T(128)} %copy-done.18, bf16[1024,768]{1,0:T(8,128)(2,1)} %get-tuple-element.143.refs_1_, ...), custom_call_target="tpu_custom_call" | custom-call | flops 103500000 | bytes 332100 | tf_op jit(solution)/shard_map/qkv_grad/pallas_call | solution.py:80
  188.8 1.5 add_convert_fusion.2.refs_16_
  190.8 1.1 collective-permute-done.30
  192.5 1.3 collective-permute-start.35
  193.8 2.6 %collective-permute-start.36 = (bf16[4,4,24,768]{3,2,1,0:T(8,128)(2,1)S(1)}, bf16[4,4,24,768]{3,2,1,0:T(8,128)(2,1)S(1)}, u32[]{:S(2)}, u32[]{:S(2)}) collective-permute-start(bf16[4,4,24,768]{3,2,1,0:T(8,128)(2,1)S(1)} %add_convert_fusion.2.refs_16_), channel_id=1, source_target_pairs={{0,16},{1,9},{2,18},{3,11},{4,20},{5,13},{6,22},{7,15},{8,24},{9,1... | collective-permute-start | bytes 1769480 | tf_op jit(solution)/shard_map/ppermute | solution.py:556
  196.6 9.2 %input_grad.1 = (bf16[1024,768]{1,0:T(8,128)(2,1)}, f32[4,1104]{1,0:T(4,128)S(1)}, f32[4,1104]{1,0:T(4,128)S(1)}, f32[8,128]{1,0:T(8,128)S(1)}) custom-call(s32[3]{0:T(128)S(1)} %copy-done.19, bf16[1024,768]{1,0:T(8,128)(2,1)S(1)} %copy-done, bf16[1024,768]{1,0:T(8,128)(2,1)S(1)} %copy-done.1, bf16[1024,384]{1,0:T(8,128)(2,1)S(1)} %copy-done.4, ...), custom_call_target="tpu_custom_call" | custom-call | flops 103500000 | bytes 332100 | tf_op jit(solution)/shard_map/input_grad/pallas_call | solution.py:80
  205.8 5.2 %collective-permute-done.36.refs_9_ = bf16[4,4,24,768]{3,2,1,0:T(8,128)(2,1)S(1)} collective-permute-done((bf16[4,4,24,768]{3,2,1,0:T(8,128)(2,1)S(1)}, bf16[4,4,24,768]{3,2,1,0:T(8,128)(2,1)S(1)}, u32[]{:S(2)}, u32[]{:S(2)}) %collective-permute-start.36) | collective-permute-done | bytes 589856 | tf_op jit(solution)/shard_map/ppermute | solution.py:556
  212.1 1.6 collective-permute-start.38
  213.7 1.2 add_convert_fusion.5.refs_7_
  214.9 1.7 collective-permute-start.39
  216.5 9.3 %output.1 = (bf16[1024,768]{1,0:T(8,128)(2,1)}, f32[8,128]{1,0:T(8,128)S(1)}) custom-call(bf16[1024,3072]{1,0:T(8,128)(2,1)} %get-tuple-element.160.refs_1_.refs_0_, f32[1024,768]{1,0:T(8,128)S(1)} %copy-done.5, f32[1,8832]{1,0:T(1,128)S(1)} %copy-done.16, bf16[3072,768]{1,0:T(8,128)(2,1)} %get-tuple-element.162.refs_3_, ...), custom_call_target="tpu_custom_call" | custom-call | flops 92000000 | bytes 295200 | tf_op jit(solution)/shard_map/output/pallas_call | solution.py:80
  226.8 1.3 collective-permute-start.43
  228.7 1.6 collective-permute-start.41
  230.3 1.1 add_convert_fusion.8
  232.1 0.9 collective-permute-done.44.refs_4_
  233.0 1.1 collective-permute-start.49
  234.2 2.3 collective-permute-start.47
  236.8 1.9 collective-permute-start.45
  239.6 2.4 collective-permute-done.49.refs_5_
  242.0 2.0 feed_sums.1
  (167 shorter events, 24.1 us)
Async XLA Ops:
  0.6 12.8 %collective-permute-start.2 = (bf16[1,24,1920]{2,1,0:T(8,128)(2,1)}, bf16[1,24,1920]{2,1,0:T(8,128)(2,1)S(1)}, u32[]{:S(2)}, u32[]{:S(2)}) collective-permute-start(bf16[1,24,1920]{2,1,0:T(8,128)(2,1)} %bitcast.30), channel_id=1, source_target_pairs={{0,24},{8,16},{16,8},{24,0},{1,25},{9,17},{17,9},{25,1},{2,26},{10... | collective-permute-start | bytes 276488 | tf_op jit(solution)/shard_map/ppermute | solution.py:560
  5.7 7.9 %collective-permute-start.1 = (bf16[1,24,1920]{2,1,0:T(8,128)(2,1)}, bf16[1,24,1920]{2,1,0:T(8,128)(2,1)S(1)}, u32[]{:S(2)}, u32[]{:S(2)}) collective-permute-start(bf16[1,24,1920]{2,1,0:T(8,128)(2,1)} %bitcast.31), channel_id=1, source_target_pairs={{0,16},{8,24},{16,0},{24,8},{1,17},{9,25},{17,1},{25,9},{2,18},{10... | collective-permute-start | bytes 276488 | tf_op jit(solution)/shard_map/ppermute | solution.py:560
  5.8 7.9 %collective-permute-start = (bf16[1,24,1920]{2,1,0:T(8,128)(2,1)}, bf16[1,24,1920]{2,1,0:T(8,128)(2,1)S(1)}, u32[]{:S(2)}, u32[]{:S(2)}) collective-permute-start(bf16[1,24,1920]{2,1,0:T(8,128)(2,1)} %bitcast.32), channel_id=1, source_target_pairs={{0,8},{8,0},{16,24},{24,16},{1,9},{9,1},{17,25},{25,17},{2,10},{10... | collective-permute-start | bytes 276488 | tf_op jit(solution)/shard_map/ppermute | solution.py:560
  7.3 5.6 %collective-permute-start.4 = (bf16[1,2,24,768]{3,2,1,0:T(8,128)(2,1)S(1)}, bf16[1,2,24,768]{3,2,1,0:T(8,128)(2,1)S(1)}, u32[]{:S(2)}, u32[]{:S(2)}) collective-permute-start(bf16[1,2,24,768]{3,2,1,0:T(8,128)(2,1)S(1)} %bitcast.35), channel_id=1, source_target_pairs={{0,4},{1,3},{2,6},{3,1},{4,0},{5,7},{6,2},{7,5},{8,12},{9,11},{10,... | collective-permute-start | bytes 221192 | tf_op jit(solution)/shard_map/ppermute | solution.py:551
  9.1 4.4 %collective-permute-start.3 = (bf16[1,2,24,768]{3,2,1,0:T(8,128)(2,1)S(1)}, bf16[1,2,24,768]{3,2,1,0:T(8,128)(2,1)S(1)}, u32[]{:S(2)}, u32[]{:S(2)}) collective-permute-start(bf16[1,2,24,768]{3,2,1,0:T(8,128)(2,1)S(1)} %bitcast.36), channel_id=1, source_target_pairs={{0,2},{1,5},{2,0},{3,7},{4,6},{5,1},{6,4},{7,3},{8,10},{9,13},{10,... | collective-permute-start | bytes 221192 | tf_op jit(solution)/shard_map/ppermute | solution.py:551
  14.7 12.1 %collective-permute-start.6 = (bf16[21,24,384]{2,1,0:T(8,128)(2,1)S(1)}, bf16[21,24,384]{2,1,0:T(8,128)(2,1)S(1)}, u32[]{:S(2)}, u32[]{:S(2)}) collective-permute-start(bf16[21,24,384]{2,1,0:T(8,128)(2,1)S(1)} %get-tuple-element.128.refs_1_), channel_id=1, source_target_pairs={{0,4},{1,3},{2,6},{3,1},{4,0},{5,7},{6,2},{7,5},{8,12},{9,11},{10,... | collective-permute-start | bytes 1161224 | tf_op jit(solution)/shard_map/ppermute | solution.py:551
  16.3 10.5 %collective-permute-start.5 = (bf16[21,24,384]{2,1,0:T(8,128)(2,1)S(1)}, bf16[21,24,384]{2,1,0:T(8,128)(2,1)S(1)}, u32[]{:S(2)}, u32[]{:S(2)}) collective-permute-start(bf16[21,24,384]{2,1,0:T(8,128)(2,1)S(1)} %get-tuple-element.128.refs_1_), channel_id=1, source_target_pairs={{0,2},{1,5},{2,0},{3,7},{4,6},{5,1},{6,4},{7,3},{8,10},{9,13},{10,... | collective-permute-start | bytes 1161224 | tf_op jit(solution)/shard_map/ppermute | solution.py:551
  17.7 9.0 %collective-permute-start.8 = (bf16[1,7,24,768]{3,2,1,0:T(8,128)(2,1)S(1)}, bf16[1,7,24,768]{3,2,1,0:T(8,128)(2,1)S(1)}, u32[]{:S(2)}, u32[]{:S(2)}) collective-permute-start(bf16[1,7,24,768]{3,2,1,0:T(8,128)(2,1)S(1)} %maximum_bitcast_fusion.1), channel_id=1, source_target_pairs={{0,8},{1,17},{2,10},{3,19},{4,12},{5,21},{6,14},{7,23},{8,0},{9,25... | collective-permute-start | bytes 774152 | tf_op jit(solution)/shard_map/ppermute | solution.py:556
  18.4 8.4 %collective-permute-start.7 = (bf16[1,2,24,768]{3,2,1,0:T(8,128)(2,1)S(1)}, bf16[1,2,24,768]{3,2,1,0:T(8,128)(2,1)S(1)}, u32[]{:S(2)}, u32[]{:S(2)}) collective-permute-start(bf16[1,2,24,768]{3,2,1,0:T(8,128)(2,1)S(1)} %collective-permute-done.3), channel_id=1, source_target_pairs={{0,4},{1,3},{2,6},{3,1},{4,0},{5,7},{6,2},{7,5},{8,12},{9,11},{10,... | collective-permute-start | bytes 221192 | tf_op jit(solution)/shard_map/ppermute | solution.py:551
  26.9 15.6 %collective-permute-start.11 = (bf16[2,7,24,768]{3,2,1,0:T(8,128)(2,1)S(1)}, bf16[2,7,24,768]{3,2,1,0:T(8,128)(2,1)S(1)}, u32[]{:S(2)}, u32[]{:S(2)}) collective-permute-start(bf16[2,7,24,768]{3,2,1,0:T(8,128)(2,1)S(1)} %constant_dynamic-update-slice_fusion), channel_id=1, source_target_pairs={{0,16},{1,9},{2,18},{3,11},{4,20},{5,13},{6,22},{7,15},{8,24},{9,1... | collective-permute-start | bytes 1548296 | tf_op jit(solution)/shard_map/ppermute | solution.py:556
  27.5 7.7 %collective-permute-start.9 = (bf16[21,24,384]{2,1,0:T(8,128)(2,1)S(1)}, bf16[21,24,384]{2,1,0:T(8,128)(2,1)S(1)}, u32[]{:S(2)}, u32[]{:S(2)}) collective-permute-start(bf16[21,24,384]{2,1,0:T(8,128)(2,1)S(1)} %collective-permute-done.5.refs_2_), channel_id=1, source_target_pairs={{0,4},{1,3},{2,6},{3,1},{4,0},{5,7},{6,2},{7,5},{8,12},{9,11},{10,... | collective-permute-start | bytes 1161224 | tf_op jit(solution)/shard_map/ppermute | solution.py:551
  44.1 18.7 %collective-permute-start.14 = (bf16[4,7,24,768]{3,2,1,0:T(8,128)(2,1)}, bf16[4,7,24,768]{3,2,1,0:T(8,128)(2,1)}, u32[]{:S(2)}, u32[]{:S(2)}) collective-permute-start(bf16[4,7,24,768]{3,2,1,0:T(8,128)(2,1)} %constant_dynamic-update-slice_fusion.2.refs_1_), channel_id=1, source_target_pairs={{0,4},{1,3},{2,6},{3,1},{4,0},{5,7},{6,2},{7,5},{8,12},{9,11},{10,... | collective-permute-start | bytes 3096584 | tf_op jit(solution)/shard_map/ppermute | solution.py:551
  45.6 17.2 %collective-permute-start.13 = (bf16[4,7,24,768]{3,2,1,0:T(8,128)(2,1)}, bf16[4,7,24,768]{3,2,1,0:T(8,128)(2,1)}, u32[]{:S(2)}, u32[]{:S(2)}) collective-permute-start(bf16[4,7,24,768]{3,2,1,0:T(8,128)(2,1)} %constant_dynamic-update-slice_fusion.2.refs_1_), channel_id=1, source_target_pairs={{0,2},{1,5},{2,0},{3,7},{4,6},{5,1},{6,4},{7,3},{8,10},{9,13},{10,... | collective-permute-start | bytes 3096584 | tf_op jit(solution)/shard_map/ppermute | solution.py:551
  46.7 2.3 collective-permute-start.17
  47.9 12.6 %collective-permute-start.12 = (bf16[1,4,2,24,768]{4,3,2,1,0:T(8,128)(2,1)S(1)}, bf16[1,4,2,24,768]{4,3,2,1,0:T(8,128)(2,1)}, u32[]{:S(2)}, u32[]{:S(2)}) collective-permute-start(bf16[1,4,2,24,768]{4,3,2,1,0:T(8,128)(2,1)S(1)} %maximum_bitcast_fusion), channel_id=1, source_target_pairs={{0,8},{1,17},{2,10},{3,19},{4,12},{5,21},{6,14},{7,23},{8,0},{9,25... | collective-permute-start | bytes 884744 | tf_op jit(solution)/shard_map/ppermute | solution.py:556
  62.8 20.5 %collective-permute-start.19 = (bf16[4,7,24,768]{3,2,1,0:T(8,128)(2,1)}, bf16[4,7,24,768]{3,2,1,0:T(8,128)(2,1)S(1)}, u32[]{:S(2)}, u32[]{:S(2)}) collective-permute-start(bf16[4,7,24,768]{3,2,1,0:T(8,128)(2,1)} %constant_dynamic-update-slice_fusion.2.refs_1_), channel_id=1, source_target_pairs={{0,1},{1,0},{2,3},{3,2},{4,5},{5,4},{6,7},{7,6},{8,9},{9,8},{10,11... | collective-permute-start | bytes 3096584 | tf_op jit(solution)/shard_map/ppermute | solution.py:564
  62.8 20.6 %collective-permute-start.21 = (bf16[4,7,24,768]{3,2,1,0:T(8,128)(2,1)}, bf16[4,7,24,768]{3,2,1,0:T(8,128)(2,1)S(1)}, u32[]{:S(2)}, u32[]{:S(2)}) collective-permute-start(bf16[4,7,24,768]{3,2,1,0:T(8,128)(2,1)} %collective-permute-done.14.refs_3_), channel_id=1, source_target_pairs={{0,1},{1,0},{2,3},{3,2},{4,5},{5,4},{6,7},{7,6},{8,9},{9,8},{10,11... | collective-permute-start | bytes 3096584 | tf_op jit(solution)/shard_map/ppermute | solution.py:564
  63.3 20.1 %collective-permute-start.20 = (bf16[4,7,24,768]{3,2,1,0:T(8,128)(2,1)}, bf16[4,7,24,768]{3,2,1,0:T(8,128)(2,1)S(1)}, u32[]{:S(2)}, u32[]{:S(2)}) collective-permute-start(bf16[4,7,24,768]{3,2,1,0:T(8,128)(2,1)} %collective-permute-done.13.refs_2_), channel_id=1, source_target_pairs={{0,1},{1,0},{2,3},{3,2},{4,5},{5,4},{6,7},{7,6},{8,9},{9,8},{10,11... | collective-permute-start | bytes 3096584 | tf_op jit(solution)/shard_map/ppermute | solution.py:564
  63.3 20.1 %collective-permute-start.18 = (bf16[4,7,24,768]{3,2,1,0:T(8,128)(2,1)}, bf16[4,7,24,768]{3,2,1,0:T(8,128)(2,1)}, u32[]{:S(2)}, u32[]{:S(2)}) collective-permute-start(bf16[4,7,24,768]{3,2,1,0:T(8,128)(2,1)} %collective-permute-done.13.refs_2_), channel_id=1, source_target_pairs={{0,4},{1,3},{2,6},{3,1},{4,0},{5,7},{6,2},{7,5},{8,12},{9,11},{10,... | collective-permute-start | bytes 3096584 | tf_op jit(solution)/shard_map/ppermute | solution.py:551
  66.1 17.3 %collective-permute-start.22 = (bf16[2,4,2,24,768]{4,3,2,1,0:T(8,128)(2,1)S(1)}, bf16[2,4,2,24,768]{4,3,2,1,0:T(8,128)(2,1)}, u32[]{:S(2)}, u32[]{:S(2)}) collective-permute-start(bf16[2,4,2,24,768]{4,3,2,1,0:T(8,128)(2,1)S(1)} %constant_dynamic-update-slice_fusion.4.refs_9_), channel_id=1, source_target_pairs={{0,16},{1,9},{2,18},{3,11},{4,20},{5,13},{6,22},{7,15},{8,24},{9,1... | collective-permute-start | bytes 1769480 | tf_op jit(solution)/shard_map/ppermute | solution.py:556
  83.4 5.7 %collective-permute-start.23 = (bf16[4,7,24,768]{3,2,1,0:T(8,128)(2,1)}, bf16[4,7,24,768]{3,2,1,0:T(8,128)(2,1)}, u32[]{:S(2)}, u32[]{:S(2)}) collective-permute-start(bf16[4,7,24,768]{3,2,1,0:T(8,128)(2,1)} %collective-permute-done.18.refs_4_), channel_id=1, source_target_pairs={{0,1},{1,0},{2,3},{3,2},{4,5},{5,4},{6,7},{7,6},{8,9},{9,8},{10,11... | collective-permute-start | bytes 3096584 | tf_op jit(solution)/shard_map/ppermute | solution.py:564
  83.5 3.9 %collective-permute-start.24 = (bf16[2,4,2,24,768]{4,3,2,1,0:T(8,128)(2,1)S(1)}, bf16[2,4,2,24,768]{4,3,2,1,0:T(8,128)(2,1)S(1)}, u32[]{:S(2)}, u32[]{:S(2)}) collective-permute-start(bf16[2,4,2,24,768]{4,3,2,1,0:T(8,128)(2,1)S(1)} %constant_dynamic-update-slice_fusion.4.refs_9_), channel_id=1, source_target_pairs={{0,1},{1,0},{2,3},{3,2},{4,5},{5,4},{6,7},{7,6},{8,9},{9,8},{10,11... | collective-permute-start | bytes 1769480 | tf_op jit(solution)/shard_map/ppermute | solution.py:564
  84.0 4.3 %collective-permute-start.25 = (bf16[2,4,2,24,768]{4,3,2,1,0:T(8,128)(2,1)}, bf16[2,4,2,24,768]{4,3,2,1,0:T(8,128)(2,1)S(1)}, u32[]{:S(2)}, u32[]{:S(2)}) collective-permute-start(bf16[2,4,2,24,768]{4,3,2,1,0:T(8,128)(2,1)} %collective-permute-done.22.refs_10_), channel_id=1, source_target_pairs={{0,1},{1,0},{2,3},{3,2},{4,5},{5,4},{6,7},{7,6},{8,9},{9,8},{10,11... | collective-permute-start | bytes 1769480 | tf_op jit(solution)/shard_map/ppermute | solution.py:564
  137.8 11.0 %collective-permute-start.26 = (bf16[8,5,24,768]{3,2,1,0:T(8,128)(2,1)}, bf16[8,5,24,768]{3,2,1,0:T(8,128)(2,1)S(1)}, u32[]{:S(2)}, u32[]{:S(2)}) collective-permute-start(bf16[8,5,24,768]{3,2,1,0:T(8,128)(2,1)} %bitcast.42), channel_id=1, source_target_pairs={{0,1},{1,0},{2,3},{3,2},{4,5},{5,4},{6,7},{7,6},{8,9},{9,8},{10,11... | collective-permute-start | bytes 4423688 | tf_op jit(solution)/shard_map/ppermute | solution.py:564
  138.2 10.6 %collective-permute-start.27 = (bf16[8,5,24,768]{3,2,1,0:T(8,128)(2,1)}, bf16[8,5,24,768]{3,2,1,0:T(8,128)(2,1)}, u32[]{:S(2)}, u32[]{:S(2)}) collective-permute-start(bf16[8,5,24,768]{3,2,1,0:T(8,128)(2,1)} %bitcast.41), channel_id=1, source_target_pairs={{0,1},{1,0},{2,3},{3,2},{4,5},{5,4},{6,7},{7,6},{8,9},{9,8},{10,11... | collective-permute-start | bytes 4423688 | tf_op jit(solution)/shard_map/ppermute | solution.py:564
  148.4 5.1 %collective-permute-start.28 = (bf16[8,4,24,768]{3,2,1,0:T(8,128)(2,1)}, bf16[8,4,24,768]{3,2,1,0:T(8,128)(2,1)S(1)}, u32[]{:S(2)}, u32[]{:S(2)}) collective-permute-start(bf16[8,4,24,768]{3,2,1,0:T(8,128)(2,1)} %get-tuple-element.177), channel_id=1, source_target_pairs={{0,1},{1,0},{2,3},{3,2},{4,5},{5,4},{6,7},{7,6},{8,9},{9,8},{10,11... | collective-permute-start | bytes 3538952 | tf_op jit(solution)/shard_map/ppermute | solution.py:564
  151.8 37.0 %collective-permute-start.31 = (bf16[8,5,24,768]{3,2,1,0:T(8,128)(2,1)}, bf16[8,5,24,768]{3,2,1,0:T(8,128)(2,1)S(1)}, u32[]{:S(2)}, u32[]{:S(2)}) collective-permute-start(bf16[8,5,24,768]{3,2,1,0:T(8,128)(2,1)} %fusion.refs_8_), channel_id=1, source_target_pairs={{0,2},{1,5},{2,0},{3,7},{4,6},{5,1},{6,4},{7,3},{8,10},{9,13},{10,... | collective-permute-start | bytes 4423688 | tf_op jit(solution)/shard_map/ppermute | solution.py:551
  154.8 33.9 %collective-permute-start.32 = (bf16[8,4,24,768]{3,2,1,0:T(8,128)(2,1)}, bf16[8,4,24,768]{3,2,1,0:T(8,128)(2,1)}, u32[]{:S(2)}, u32[]{:S(2)}) collective-permute-start(bf16[8,4,24,768]{3,2,1,0:T(8,128)(2,1)} %add_convert_fusion.refs_9_), channel_id=1, source_target_pairs={{0,8},{1,17},{2,10},{3,19},{4,12},{5,21},{6,14},{7,23},{8,0},{9,25... | collective-permute-start | bytes 3538952 | tf_op jit(solution)/shard_map/ppermute | solution.py:556
  154.9 33.9 %collective-permute-start.33 = (bf16[8,4,24,768]{3,2,1,0:T(8,128)(2,1)}, bf16[8,4,24,768]{3,2,1,0:T(8,128)(2,1)}, u32[]{:S(2)}, u32[]{:S(2)}) collective-permute-start(bf16[8,4,24,768]{3,2,1,0:T(8,128)(2,1)} %get-tuple-element.197), channel_id=1, source_target_pairs={{0,1},{1,0},{2,3},{3,2},{4,5},{5,4},{6,7},{7,6},{8,9},{9,8},{10,11... | collective-permute-start | bytes 3538952 | tf_op jit(solution)/shard_map/ppermute | solution.py:564
  188.1 2.6 %collective-permute-start.29 = (bf16[8,5,24,384]{3,2,1,0:T(8,128)(2,1)}, bf16[8,5,24,384]{3,2,1,0:T(8,128)(2,1)S(1)}, u32[]{:S(2)}, u32[]{:S(2)}) collective-permute-start(bf16[8,5,24,384]{3,2,1,0:T(8,128)(2,1)} %get-tuple-element.191), channel_id=1, source_target_pairs={{0,1},{1,0},{2,3},{3,2},{4,5},{5,4},{6,7},{7,6},{8,9},{9,8},{10,11... | collective-permute-start | bytes 2211848 | tf_op jit(solution)/shard_map/ppermute | solution.py:564
  188.7 3.1 %collective-permute-start.30 = (bf16[8,5,24,384]{3,2,1,0:T(8,128)(2,1)}, bf16[8,5,24,384]{3,2,1,0:T(8,128)(2,1)S(1)}, u32[]{:S(2)}, u32[]{:S(2)}) collective-permute-start(bf16[8,5,24,384]{3,2,1,0:T(8,128)(2,1)} %get-tuple-element.192), channel_id=1, source_target_pairs={{0,1},{1,0},{2,3},{3,2},{4,5},{5,4},{6,7},{7,6},{8,9},{9,8},{10,11... | collective-permute-start | bytes 2211848 | tf_op jit(solution)/shard_map/ppermute | solution.py:564
  192.0 19.0 %collective-permute-start.34 = (bf16[8,5,24,384]{3,2,1,0:T(8,128)(2,1)S(1)}, bf16[8,5,24,384]{3,2,1,0:T(8,128)(2,1)S(1)}, u32[]{:S(2)}, u32[]{:S(2)}) collective-permute-start(bf16[8,5,24,384]{3,2,1,0:T(8,128)(2,1)S(1)} %add_convert_fusion.1.refs_14_), channel_id=1, source_target_pairs={{0,2},{1,5},{2,0},{3,7},{4,6},{5,1},{6,4},{7,3},{8,10},{9,13},{10,... | collective-permute-start | bytes 2211848 | tf_op jit(solution)/shard_map/ppermute | solution.py:551
  192.5 18.5 %collective-permute-start.35 = (bf16[4,5,24,768]{3,2,1,0:T(8,128)(2,1)S(1)}, bf16[4,5,24,768]{3,2,1,0:T(8,128)(2,1)S(1)}, u32[]{:S(2)}, u32[]{:S(2)}) collective-permute-start(bf16[4,5,24,768]{3,2,1,0:T(8,128)(2,1)S(1)} %fusion.2.refs_15_), channel_id=1, source_target_pairs={{0,4},{1,3},{2,6},{3,1},{4,0},{5,7},{6,2},{7,5},{8,12},{9,11},{10,... | collective-permute-start | bytes 2211848 | tf_op jit(solution)/shard_map/ppermute | solution.py:551
  193.8 17.1 %collective-permute-start.36 = (bf16[4,4,24,768]{3,2,1,0:T(8,128)(2,1)S(1)}, bf16[4,4,24,768]{3,2,1,0:T(8,128)(2,1)S(1)}, u32[]{:S(2)}, u32[]{:S(2)}) collective-permute-start(bf16[4,4,24,768]{3,2,1,0:T(8,128)(2,1)S(1)} %add_convert_fusion.2.refs_16_), channel_id=1, source_target_pairs={{0,16},{1,9},{2,18},{3,11},{4,20},{5,13},{6,22},{7,15},{8,24},{9,1... | collective-permute-start | bytes 1769480 | tf_op jit(solution)/shard_map/ppermute | solution.py:556
  211.1 14.7 %collective-permute-start.37 = (bf16[4,5,24,384]{3,2,1,0:T(8,128)(2,1)S(1)}, bf16[4,5,24,384]{3,2,1,0:T(8,128)(2,1)S(1)}, u32[]{:S(2)}, u32[]{:S(2)}) collective-permute-start(bf16[4,5,24,384]{3,2,1,0:T(8,128)(2,1)S(1)} %add_convert_fusion.4.refs_5_), channel_id=1, source_target_pairs={{0,4},{1,3},{2,6},{3,1},{4,0},{5,7},{6,2},{7,5},{8,12},{9,11},{10,... | collective-permute-start | bytes 1105928 | tf_op jit(solution)/shard_map/ppermute | solution.py:551
  212.1 13.7 %collective-permute-start.38 = (bf16[2,5,24,768]{3,2,1,0:T(8,128)(2,1)S(1)}, bf16[2,5,24,768]{3,2,1,0:T(8,128)(2,1)S(1)}, u32[]{:S(2)}, u32[]{:S(2)}) collective-permute-start(bf16[2,5,24,768]{3,2,1,0:T(8,128)(2,1)S(1)} %add_convert_fusion.3.refs_6_), channel_id=1, source_target_pairs={{0,8},{1,17},{2,10},{3,19},{4,12},{5,21},{6,14},{7,23},{8,0},{9,25... | collective-permute-start | bytes 1105928 | tf_op jit(solution)/shard_map/ppermute | solution.py:556
  214.9 11.0 %collective-permute-start.39 = (bf16[2,4,24,768]{3,2,1,0:T(8,128)(2,1)S(1)}, bf16[2,4,24,768]{3,2,1,0:T(8,128)(2,1)S(1)}, u32[]{:S(2)}, u32[]{:S(2)}) collective-permute-start(bf16[2,4,24,768]{3,2,1,0:T(8,128)(2,1)S(1)} %add_convert_fusion.5.refs_7_), channel_id=1, source_target_pairs={{0,2},{1,5},{2,0},{3,7},{4,6},{5,1},{6,4},{7,3},{8,10},{9,13},{10,... | collective-permute-start | bytes 884744 | tf_op jit(solution)/shard_map/ppermute | solution.py:551
  216.5 9.3 %collective-permute-start.40 = (f32[4,1104]{1,0:T(4,128)S(1)}, f32[4,1104]{1,0:T(4,128)S(1)}, u32[]{:S(2)}, u32[]{:S(2)}) collective-permute-start(f32[4,1104]{1,0:T(4,128)S(1)} %get-tuple-element.212), channel_id=1, source_target_pairs={{0,1},{1,0},{2,3},{3,2},{4,5},{5,4},{6,7},{7,6},{8,9},{9,8},{10,11... | collective-permute-start | bytes 53000 | tf_op jit(solution)/shard_map/ppermute | solution.py:564
  226.0 7.1 %collective-permute-start.44 = (bf16[2,5,24,384]{3,2,1,0:T(8,128)(2,1)S(1)}, bf16[2,5,24,384]{3,2,1,0:T(8,128)(2,1)S(1)}, u32[]{:S(2)}, u32[]{:S(2)}) collective-permute-start(bf16[2,5,24,384]{3,2,1,0:T(8,128)(2,1)S(1)} %add_convert_fusion.7), channel_id=1, source_target_pairs={{0,8},{1,17},{2,10},{3,19},{4,12},{5,21},{6,14},{7,23},{8,0},{9,25... | collective-permute-start | bytes 552968 | tf_op jit(solution)/shard_map/ppermute | solution.py:556
  226.8 7.4 %collective-permute-start.43 = (f32[1104]{0:T(1024)S(1)}, f32[1104]{0:T(1024)S(1)}, u32[]{:S(2)}, u32[]{:S(2)}) collective-permute-start(f32[1104]{0:T(1024)S(1)} %get-tuple-element.232), channel_id=1, source_target_pairs={{0,6},{1,7},{2,4},{3,5},{4,2},{5,3},{6,0},{7,1},{8,14},{9,15},{10,... | collective-permute-start | bytes 13256 | tf_op jit(solution)/shard_map/ppermute | solution.py:564
  228.0 6.2 %collective-permute-start.42 = (f32[1104]{0:T(1024)S(1)}, f32[1104]{0:T(1024)S(1)}, u32[]{:S(2)}, u32[]{:S(2)}) collective-permute-start(f32[1104]{0:T(1024)S(1)} %get-tuple-element.233), channel_id=1, source_target_pairs={{0,4},{1,5},{2,6},{3,7},{4,0},{5,1},{6,2},{7,3},{8,12},{9,13},{10,... | collective-permute-start | bytes 13256 | tf_op jit(solution)/shard_map/ppermute | solution.py:564
  228.7 5.5 %collective-permute-start.41 = (f32[1104]{0:T(1024)S(1)}, f32[1104]{0:T(1024)S(1)}, u32[]{:S(2)}, u32[]{:S(2)}) collective-permute-start(f32[1104]{0:T(1024)S(1)} %get-tuple-element.234), channel_id=1, source_target_pairs={{0,2},{1,3},{2,0},{3,1},{4,6},{5,7},{6,4},{7,5},{8,10},{9,11},{10,... | collective-permute-start | bytes 13256 | tf_op jit(solution)/shard_map/ppermute | solution.py:564
  231.4 7.3 %collective-permute-start.50 = (bf16[1,4,24,768]{3,2,1,0:T(8,128)(2,1)S(1)}, bf16[1,4,24,768]{3,2,1,0:T(8,128)(2,1)S(1)}, u32[]{:S(2)}, u32[]{:S(2)}) collective-permute-start(bf16[1,4,24,768]{3,2,1,0:T(8,128)(2,1)S(1)} %add_convert_fusion.8), channel_id=1, source_target_pairs={{0,4},{1,3},{2,6},{3,1},{4,0},{5,7},{6,2},{7,5},{8,12},{9,11},{10,... | collective-permute-start | bytes 442376 | tf_op jit(solution)/shard_map/ppermute | solution.py:551
  233.0 9.0 %collective-permute-start.49 = (bf16[1,5,24,768]{3,2,1,0:T(8,128)(2,1)S(1)}, bf16[1,5,24,768]{3,2,1,0:T(8,128)(2,1)S(1)}, u32[]{:S(2)}, u32[]{:S(2)}) collective-permute-start(bf16[1,5,24,768]{3,2,1,0:T(8,128)(2,1)S(1)} %add_convert_fusion.6), channel_id=1, source_target_pairs={{0,16},{1,9},{2,18},{3,11},{4,20},{5,13},{6,22},{7,15},{8,24},{9,1... | collective-permute-start | bytes 552968 | tf_op jit(solution)/shard_map/ppermute | solution.py:556
  234.2 9.7 %collective-permute-start.47 = (f32[1104]{0:T(1024)S(1)}, f32[1104]{0:T(1024)S(1)}, u32[]{:S(2)}, u32[]{:S(2)}) collective-permute-start(f32[1104]{0:T(1024)S(1)} %add_add_fusion.1), channel_id=1, source_target_pairs={{0,24},{8,16},{16,8},{24,0},{1,25},{9,17},{17,9},{25,1},{2,26},{10... | collective-permute-start | bytes 13256 | tf_op jit(solution)/shard_map/ppermute | solution.py:560
  236.5 7.4 %collective-permute-start.46 = (f32[1104]{0:T(1024)S(1)}, f32[1104]{0:T(1024)S(1)}, u32[]{:S(2)}, u32[]{:S(2)}) collective-permute-start(f32[1104]{0:T(1024)S(1)} %add_add_fusion.1), channel_id=1, source_target_pairs={{0,16},{8,24},{16,0},{24,8},{1,17},{9,25},{17,1},{25,9},{2,18},{10... | collective-permute-start | bytes 13256 | tf_op jit(solution)/shard_map/ppermute | solution.py:560
  236.8 7.1 %collective-permute-start.45 = (f32[1104]{0:T(1024)S(1)}, f32[1104]{0:T(1024)S(1)}, u32[]{:S(2)}, u32[]{:S(2)}) collective-permute-start(f32[1104]{0:T(1024)S(1)} %add_add_fusion.1), channel_id=1, source_target_pairs={{0,8},{8,0},{16,24},{24,16},{1,9},{9,1},{17,25},{25,17},{2,10},{10... | collective-permute-start | bytes 13256 | tf_op jit(solution)/shard_map/ppermute | solution.py:560
  238.7 6.0 %collective-permute-start.48 = (bf16[1,5,24,384]{3,2,1,0:T(8,128)(2,1)S(1)}, bf16[1,5,24,384]{3,2,1,0:T(8,128)(2,1)S(1)}, u32[]{:S(2)}, u32[]{:S(2)}) collective-permute-start(bf16[1,5,24,384]{3,2,1,0:T(8,128)(2,1)S(1)} %add_convert_fusion.9), channel_id=1, source_target_pairs={{0,16},{1,9},{2,18},{3,11},{4,20},{5,13},{6,22},{7,15},{8,24},{9,1... | collective-permute-start | bytes 276488 | tf_op jit(solution)/shard_map/ppermute | solution.py:556
  (39 other events, 277.6 us)

commit v2 on v1

--- a/solution.py
+++ b/solution.py
@@ -355,7 +355,7 @@
     )
 
 
-def feed_kernel(*refs, pieces, chunk=512):
+def feed_kernel(*refs, pieces, chunk=256):
     if pieces:
         where_ref, *side = refs[: pieces + 1]
         (
@@ -381,15 +381,22 @@
     a_ref[...] = a
     c = c_ref[...]
     da = jnp.zeros(x1.shape, F32)
-    for s in range(0, wu_ref.shape[1], chunk):
-        at = slice(s, s + chunk)
-        u = nn(a, wu_ref[:, at]) + bu_ref[:, at]
-        dy = nt(c, wd_ref[at])
+    spans = [slice(n, n + chunk) for n in range(0, wu_ref.shape[1], chunk)]
+
+    def products(at):
+        return nn(a, wu_ref[:, at]) + bu_ref[:, at], nt(c, wd_ref[at])
+
+    ahead = products(spans[0])
+    for i, at in enumerate(spans):
+        u, dy = ahead
+        if i + 1 < len(spans):
+            ahead = products(spans[i + 1])
         u2 = u * u
         t = jnp.tanh(u * (GELU + (GELU * CUBE) * u2))
         h = 0.5 * t + 0.5
-        y_ref[:, at] = (u * h).astype(BF)
-        slope = h + (0.5 * u) * (1.0 - t * t) * (GELU + (3 * GELU * CUBE) * u2)
+        y = u * h
+        y_ref[:, at] = y.astype(BF)
+        slope = h + (y - y * h) * (2 * GELU + (6 * GELU * CUBE) * u2)
         du = (slope * dy).astype(BF)
         du_ref[:, at] = du
         dbu_ref[:, at] += column_sum(du)

time: 246 us -> 245 us (level)
  no operation moved by 1% of the time
where the time goes in v2:
time: 245 us; the launch traced here: 244 us
  Pallas kernels  136 us (56%)
  starting transfers between devices  45.1 us (18%)
  waiting for transfers between devices  42 us (17%)
  other arithmetic  10.7 us (4%)
  local copies, waits for them, and re-layouts  9.2 us (4%)
    pallas_call x13, Pallas kernels, call(): pl.pallas_call(body, grid_spec=pltpu.PrefetchScalarGridSpec(num_scalar_pr...  136 us
    ppermute x15, starting transfers between devices, plane_step(): lax.ppermute(v, 'fsdp', [(i, i ^ (2 if i % 2 == step else 4)) for i in ra...  18.5 us
    ppermute x10, waiting for transfers between devices, depth_step(): return lax.ppermute(v, AXES, pairs)  18.1 us
    ppermute x15, waiting for transfers between devices, plane_step(): lax.ppermute(v, 'fsdp', [(i, i ^ (2 if i % 2 == step else 4)) for i in ra...  16.3 us
    ppermute x6, starting transfers between devices, depth_swap(): return lax.ppermute(v, 'dp', [(i, i ^ bits) for i in range(4)])  10.2 us
    ppermute x10, starting transfers between devices, depth_step(): return lax.ppermute(v, AXES, pairs)  9.56 us
    ppermute x20, waiting for transfers between devices, fsdp_swap(): return lax.ppermute(v, 'fsdp', [(i, i ^ bit) for i in range(8)])  7.27 us
    ppermute x20, starting transfers between devices, fsdp_swap(): return lax.ppermute(v, 'fsdp', [(i, i ^ bit) for i in range(8)])  6.83 us
  transfers between devices with their start and end apart: 51, of which 17 were waited for; matrix products, arithmetic and copies ran while one was open for 6% of the time, Pallas kernels for 36%

profile of v2, /device:TPU:0, one launch (start us, length us, event | category | flops | bytes accessed | tf_op | source)
XLA Modules:
  0.0 243.7 jit_solution(17060359820772186688)
XLA Ops:
  0.6 5.1 %collective-permute-start.2 = (bf16[1,24,1920]{2,1,0:T(8,128)(2,1)}, bf16[1,24,1920]{2,1,0:T(8,128)(2,1)S(1)}, u32[]{:S(2)}, u32[]{:S(2)}) collective-permute-start(bf16[1,24,1920]{2,1,0:T(8,128)(2,1)} %bitcast.30), channel_id=1, source_target_pairs={{0,24},{8,16},{16,8},{24,0},{1,25},{9,17},{17,9},{25,1},{2,26},{10... | collective-permute-start | bytes 276488 | tf_op jit(solution)/shard_map/ppermute | solution.py:567
  6.4 0.9 fusion.3
  7.3 1.7 collective-permute-start.4
  9.1 1.5 collective-permute-start.3
  11.2 0.9 copy.20
  14.7 1.6 collective-permute-start.6
  16.3 1.5 collective-permute-start.5
  19.2 7.6 %collective-permute-done.7 = bf16[1,2,24,768]{3,2,1,0:T(8,128)(2,1)S(1)} collective-permute-done((bf16[1,2,24,768]{3,2,1,0:T(8,128)(2,1)S(1)}, bf16[1,2,24,768]{3,2,1,0:T(8,128)(2,1)S(1)}, u32[]{:S(2)}, u32[]{:S(2)}) %collective-permute-start.7) | collective-permute-done | bytes 73760 | tf_op jit(solution)/shard_map/ppermute | solution.py:558
  27.5 1.1 collective-permute-start.9
  29.2 6.0 %collective-permute-done.9.refs_4_ = bf16[21,24,384]{2,1,0:T(8,128)(2,1)S(1)} collective-permute-done((bf16[21,24,384]{2,1,0:T(8,128)(2,1)S(1)}, bf16[21,24,384]{2,1,0:T(8,128)(2,1)S(1)}, u32[]{:S(2)}, u32[]{:S(2)}) %collective-permute-start.9) | collective-permute-done | bytes 387104 | tf_op jit(solution)/shard_map/ppermute | solution.py:558
  35.2 7.2 %collective-permute-done.11 = bf16[2,7,24,768]{3,2,1,0:T(8,128)(2,1)S(1)} collective-permute-done((bf16[2,7,24,768]{3,2,1,0:T(8,128)(2,1)S(1)}, bf16[2,7,24,768]{3,2,1,0:T(8,128)(2,1)S(1)}, u32[]{:S(2)}, u32[]{:S(2)}) %collective-permute-start.11) | collective-permute-done | bytes 516128 | tf_op jit(solution)/shard_map/ppermute | solution.py:563
  44.1 1.5 collective-permute-start.14
  46.7 1.2 collective-permute-done.16.refs_7_
  50.9 9.5 %project.1 = (bf16[1024,768]{1,0:T(8,128)(2,1)}, bf16[1024,768]{1,0:T(8,128)(2,1)}, bf16[1024,768]{1,0:T(8,128)(2,1)}, bf16[1024,768]{1,0:T(8,128)(2,1)}, bf16[768,1920]{1,0:T(8,128)(2,1)}, /*index=5*/f32[8,128]{1,0:T(8,128)}) custom-call(s32[3]{0:T(128)} %copy-done.18, bf16[21,24,384]{2,1,0:T(8,128)(2,1)} %copy-done.7, bf16[21,24,384]{2,1,0:T(8,128)(2,1)} %copy-done.9, ...), custom_call_target="tpu_custom_call" | custom-call | flops 92000000 | bytes 295200 | tf_op jit(solution)/shard_map/project/pallas_call | solution.py:80
  60.5 2.3 collective-permute-done.14.refs_3_
  63.3 1.7 collective-permute-start.18
  65.1 1.0 constant_dynamic-update-slice_fusion.4.refs_9_
  66.1 1.3 collective-permute-start.22
  67.3 13.8 %attend_forward.1 = (bf16[1024,768]{1,0:T(8,128)(2,1)}, f32[6,2,1024]{2,1,0:T(2,128)}, f32[8,128]{1,0:T(8,128)}) custom-call(s32[1,2]{1,0:T(1,128)} %refs_0_.3, bf16[1024,768]{1,0:T(8,128)(2,1)} %get-tuple-element.149.refs_1_, bf16[1024,768]{1,0:T(8,128)(2,1)} %get-tuple-element.150.refs_2_, bf16[1024,768]{1,0:T(8,128)(2,1)} %get-tuple-element.151.refs_3_, ...), custom_call_target="tpu_custom_call" | custom-call | flops 241500000 | bytes 774900 | tf_op jit(solution)/shard_map/attend_forward/pallas_call | solution.py:80
  81.2 2.2 collective-permute-done.22.refs_10_
  84.1 3.4 %collective-permute-done.24.refs_11_ = bf16[2,4,2,24,768]{4,3,2,1,0:T(8,128)(2,1)S(1)} collective-permute-done((bf16[2,4,2,24,768]{4,3,2,1,0:T(8,128)(2,1)S(1)}, bf16[2,4,2,24,768]{4,3,2,1,0:T(8,128)(2,1)S(1)}, u32[]{:S(2)}, u32[]{:S(2)}) %collective-permute-start.24) | collective-permute-done | bytes 589856 | tf_op jit(solution)/shard_map/ppermute | solution.py:571
  89.1 33.7 %feed_forward.1 = (f32[1024,768]{1,0:T(8,128)}, bf16[1024,768]{1,0:T(8,128)(2,1)}, bf16[1024,3072]{1,0:T(8,128)(2,1)}, bf16[1024,3072]{1,0:T(8,128)(2,1)}, f32[1...) custom-call(s32[3]{0:T(128)} %copy-done.18, ...), custom_call_target="tpu_custom_call" | custom-call | flops 356500000 | bytes 1143900 | tf_op jit(solution)/shard_map/feed_forward/pallas_call | solution.py:80
  122.8 13.2 %down_out_grad.1 = (bf16[2,4,5,24,768]{4,3,2,1,0:T(8,128)(2,1)}, bf16[2,4,5,24,768]{4,3,2,1,0:T(8,128)(2,1)}, bf16[2,4,5,24,768]{4,3,2,1,0:T(8,128)(2,1)}, bf16[2,4,5,24,768]{4,3,2,1,0:T(8,128)(2,1)}, f32[8,128]{1,0:T(8,128)}) custom-call(s32[3]{0:T(128)} %copy-done.18, bf16[1024,3072]{1,0:T(8,128)(2,1)} %get-tuple-element.160.refs_1_.refs_0_, ...), custom_call_target="tpu_custom_call" | custom-call | flops 143750000 | bytes 461250 | tf_op jit(solution)/shard_map/down_out_grad/pallas_call | solution.py:80
  136.6 10.0 %up_grad.1 = (bf16[8,4,24,768]{3,2,1,0:T(8,128)(2,1)}, bf16[8,4,24,768]{3,2,1,0:T(8,128)(2,1)}, bf16[8,4,24,768]{3,2,1,0:T(8,128)(2,1)}, bf16[8,4,24,768]{3,2,1,0:T(8,128)(2,1)}, f32[8,128]{1,0:T(8,128)}) custom-call(s32[3]{0:T(128)} %copy-done.18, bf16[1024,768]{1,0:T(8,128)(2,1)} %get-tuple-element.165.refs_1_, ...), custom_call_target="tpu_custom_call" | custom-call | flops 103500000 | bytes 332100 | tf_op jit(solution)/shard_map/up_grad/pallas_call | solution.py:80
  147.0 2.9 %fusion.refs_8_ = bf16[8,5,24,768]{3,2,1,0:T(8,128)(2,1)} fusion(bf16[8,5,24,768]{3,2,1,0:T(8,128)(2,1)} %collective-permute-done.27, bf16[2,4,5,24,768]{4,3,2,1,0:T(8,128)(2,1)S(1)} %copy-done.27), kind=kLoop, calls=%fused_computation.1 | loop fusion | flops 2949120 | bytes 4423680 | tf_op jit(solution)/shard_map/convert_element_type | solution.py:668
  150.0 1.7 collective-permute-start.31
  151.7 1.3 add_convert_fusion.refs_9_
  153.1 23.7 %attend_backward.1 = (bf16[1024,768]{1,0:T(8,128)(2,1)}, bf16[1024,768]{1,0:T(8,128)(2,1)}, bf16[1024,384]{1,0:T(8,128)(2,1)}, bf16[1024,384]{1,0:T(8,128)(2,1)}, f32[8,128]{1,0:T(8,128)}) custom-call(s32[1,2]{1,0:T(1,128)} %refs_0_.3, bf16[1024,768]{1,0:T(8,128)(2,1)} %get-tuple-element.149.refs_1_, bf16[1024,768]{1,0:T(8,128)(2,1)} %get-tuple-element.150.refs_2_, ...), custom_call_target="tpu_custom_call" | custom-call | flops 414000000 | bytes 1328400 | tf_op jit(solution)/shard_map/attend_backward/pallas_call | solution.py:80
  176.7 9.6 %qkv_grad.1 = (bf16[8,5,24,384]{3,2,1,0:T(8,128)(2,1)}, bf16[8,5,24,384]{3,2,1,0:T(8,128)(2,1)}, bf16[8,5,24,384]{3,2,1,0:T(8,128)(2,1)}, bf16[8,5,24,384]{3,2,1,0:T(8,128)(2,1)}, f32[8,128]{1,0:T(8,128)}) custom-call(s32[3]{0:T(128)} %copy-done.18, bf16[1024,768]{1,0:T(8,128)(2,1)} %get-tuple-element.143.refs_1_, ...), custom_call_target="tpu_custom_call" | custom-call | flops 103500000 | bytes 332100 | tf_op jit(solution)/shard_map/qkv_grad/pallas_call | solution.py:80
  187.0 1.5 add_convert_fusion.2.refs_16_
  189.0 1.1 collective-permute-done.30
  190.7 1.3 collective-permute-start.35
  192.0 2.6 %collective-permute-start.36 = (bf16[4,4,24,768]{3,2,1,0:T(8,128)(2,1)S(1)}, bf16[4,4,24,768]{3,2,1,0:T(8,128)(2,1)S(1)}, u32[]{:S(2)}, u32[]{:S(2)}) collective-permute-start(bf16[4,4,24,768]{3,2,1,0:T(8,128)(2,1)S(1)} %add_convert_fusion.2.refs_16_), channel_id=1, source_target_pairs={{0,16},{1,9},{2,18},{3,11},{4,20},{5,13},{6,22},{7,15},{8,24},{9,1... | collective-permute-start | bytes 1769480 | tf_op jit(solution)/shard_map/ppermute | solution.py:563
  194.8 9.2 %input_grad.1 = (bf16[1024,768]{1,0:T(8,128)(2,1)}, f32[4,1104]{1,0:T(4,128)S(1)}, f32[4,1104]{1,0:T(4,128)S(1)}, f32[8,128]{1,0:T(8,128)S(1)}) custom-call(s32[3]{0:T(128)S(1)} %copy-done.19, bf16[1024,768]{1,0:T(8,128)(2,1)S(1)} %copy-done, bf16[1024,768]{1,0:T(8,128)(2,1)S(1)} %copy-done.1, bf16[1024,384]{1,0:T(8,128)(2,1)S(1)} %copy-done.4, ...), custom_call_target="tpu_custom_call" | custom-call | flops 103500000 | bytes 332100 | tf_op jit(solution)/shard_map/input_grad/pallas_call | solution.py:80
  204.0 5.2 %collective-permute-done.36.refs_9_ = bf16[4,4,24,768]{3,2,1,0:T(8,128)(2,1)S(1)} collective-permute-done((bf16[4,4,24,768]{3,2,1,0:T(8,128)(2,1)S(1)}, bf16[4,4,24,768]{3,2,1,0:T(8,128)(2,1)S(1)}, u32[]{:S(2)}, u32[]{:S(2)}) %collective-permute-start.36) | collective-permute-done | bytes 589856 | tf_op jit(solution)/shard_map/ppermute | solution.py:563
  210.3 1.5 collective-permute-start.38
  211.9 1.2 add_convert_fusion.5.refs_7_
  213.1 1.7 collective-permute-start.39
  214.7 9.3 %output.1 = (bf16[1024,768]{1,0:T(8,128)(2,1)}, f32[8,128]{1,0:T(8,128)S(1)}) custom-call(bf16[1024,3072]{1,0:T(8,128)(2,1)} %get-tuple-element.160.refs_1_.refs_0_, f32[1024,768]{1,0:T(8,128)S(1)} %copy-done.5, f32[1,8832]{1,0:T(1,128)S(1)} %copy-done.16, bf16[3072,768]{1,0:T(8,128)(2,1)} %get-tuple-element.162.refs_3_, ...), custom_call_target="tpu_custom_call" | custom-call | flops 92000000 | bytes 295200 | tf_op jit(solution)/shard_map/output/pallas_call | solution.py:80
  225.0 1.3 collective-permute-start.43
  226.9 1.6 collective-permute-start.41
  228.5 1.1 add_convert_fusion.8
  230.3 0.9 collective-permute-done.44.refs_4_
  231.2 1.1 collective-permute-start.49
  232.4 2.3 collective-permute-start.47
  235.0 1.9 collective-permute-start.45
  237.8 2.4 collective-permute-done.49.refs_5_
  240.2 2.0 feed_sums.1
  (167 shorter events, 24.1 us)
Async XLA Ops:
  0.6 12.8 %collective-permute-start.2 = (bf16[1,24,1920]{2,1,0:T(8,128)(2,1)}, bf16[1,24,1920]{2,1,0:T(8,128)(2,1)S(1)}, u32[]{:S(2)}, u32[]{:S(2)}) collective-permute-start(bf16[1,24,1920]{2,1,0:T(8,128)(2,1)} %bitcast.30), channel_id=1, source_target_pairs={{0,24},{8,16},{16,8},{24,0},{1,25},{9,17},{17,9},{25,1},{2,26},{10... | collective-permute-start | bytes 276488 | tf_op jit(solution)/shard_map/ppermute | solution.py:567
  5.7 7.9 %collective-permute-start.1 = (bf16[1,24,1920]{2,1,0:T(8,128)(2,1)}, bf16[1,24,1920]{2,1,0:T(8,128)(2,1)S(1)}, u32[]{:S(2)}, u32[]{:S(2)}) collective-permute-start(bf16[1,24,1920]{2,1,0:T(8,128)(2,1)} %bitcast.31), channel_id=1, source_target_pairs={{0,16},{8,24},{16,0},{24,8},{1,17},{9,25},{17,1},{25,9},{2,18},{10... | collective-permute-start | bytes 276488 | tf_op jit(solution)/shard_map/ppermute | solution.py:567
  5.8 7.9 %collective-permute-start = (bf16[1,24,1920]{2,1,0:T(8,128)(2,1)}, bf16[1,24,1920]{2,1,0:T(8,128)(2,1)S(1)}, u32[]{:S(2)}, u32[]{:S(2)}) collective-permute-start(bf16[1,24,1920]{2,1,0:T(8,128)(2,1)} %bitcast.32), channel_id=1, source_target_pairs={{0,8},{8,0},{16,24},{24,16},{1,9},{9,1},{17,25},{25,17},{2,10},{10... | collective-permute-start | bytes 276488 | tf_op jit(solution)/shard_map/ppermute | solution.py:567
  7.3 5.6 %collective-permute-start.4 = (bf16[1,2,24,768]{3,2,1,0:T(8,128)(2,1)S(1)}, bf16[1,2,24,768]{3,2,1,0:T(8,128)(2,1)S(1)}, u32[]{:S(2)}, u32[]{:S(2)}) collective-permute-start(bf16[1,2,24,768]{3,2,1,0:T(8,128)(2,1)S(1)} %bitcast.35), channel_id=1, source_target_pairs={{0,4},{1,3},{2,6},{3,1},{4,0},{5,7},{6,2},{7,5},{8,12},{9,11},{10,... | collective-permute-start | bytes 221192 | tf_op jit(solution)/shard_map/ppermute | solution.py:558
  9.1 4.4 %collective-permute-start.3 = (bf16[1,2,24,768]{3,2,1,0:T(8,128)(2,1)S(1)}, bf16[1,2,24,768]{3,2,1,0:T(8,128)(2,1)S(1)}, u32[]{:S(2)}, u32[]{:S(2)}) collective-permute-start(bf16[1,2,24,768]{3,2,1,0:T(8,128)(2,1)S(1)} %bitcast.36), channel_id=1, source_target_pairs={{0,2},{1,5},{2,0},{3,7},{4,6},{5,1},{6,4},{7,3},{8,10},{9,13},{10,... | collective-permute-start | bytes 221192 | tf_op jit(solution)/shard_map/ppermute | solution.py:558
  14.7 12.1 %collective-permute-start.6 = (bf16[21,24,384]{2,1,0:T(8,128)(2,1)S(1)}, bf16[21,24,384]{2,1,0:T(8,128)(2,1)S(1)}, u32[]{:S(2)}, u32[]{:S(2)}) collective-permute-start(bf16[21,24,384]{2,1,0:T(8,128)(2,1)S(1)} %get-tuple-element.128.refs_1_), channel_id=1, source_target_pairs={{0,4},{1,3},{2,6},{3,1},{4,0},{5,7},{6,2},{7,5},{8,12},{9,11},{10,... | collective-permute-start | bytes 1161224 | tf_op jit(solution)/shard_map/ppermute | solution.py:558
  16.3 10.5 %collective-permute-start.5 = (bf16[21,24,384]{2,1,0:T(8,128)(2,1)S(1)}, bf16[21,24,384]{2,1,0:T(8,128)(2,1)S(1)}, u32[]{:S(2)}, u32[]{:S(2)}) collective-permute-start(bf16[21,24,384]{2,1,0:T(8,128)(2,1)S(1)} %get-tuple-element.128.refs_1_), channel_id=1, source_target_pairs={{0,2},{1,5},{2,0},{3,7},{4,6},{5,1},{6,4},{7,3},{8,10},{9,13},{10,... | collective-permute-start | bytes 1161224 | tf_op jit(solution)/shard_map/ppermute | solution.py:558
  17.7 9.0 %collective-permute-start.8 = (bf16[1,7,24,768]{3,2,1,0:T(8,128)(2,1)S(1)}, bf16[1,7,24,768]{3,2,1,0:T(8,128)(2,1)S(1)}, u32[]{:S(2)}, u32[]{:S(2)}) collective-permute-start(bf16[1,7,24,768]{3,2,1,0:T(8,128)(2,1)S(1)} %maximum_bitcast_fusion.1), channel_id=1, source_target_pairs={{0,8},{1,17},{2,10},{3,19},{4,12},{5,21},{6,14},{7,23},{8,0},{9,25... | collective-permute-start | bytes 774152 | tf_op jit(solution)/shard_map/ppermute | solution.py:563
  18.4 8.4 %collective-permute-start.7 = (bf16[1,2,24,768]{3,2,1,0:T(8,128)(2,1)S(1)}, bf16[1,2,24,768]{3,2,1,0:T(8,128)(2,1)S(1)}, u32[]{:S(2)}, u32[]{:S(2)}) collective-permute-start(bf16[1,2,24,768]{3,2,1,0:T(8,128)(2,1)S(1)} %collective-permute-done.3), channel_id=1, source_target_pairs={{0,4},{1,3},{2,6},{3,1},{4,0},{5,7},{6,2},{7,5},{8,12},{9,11},{10,... | collective-permute-start | bytes 221192 | tf_op jit(solution)/shard_map/ppermute | solution.py:558
  26.9 15.6 %collective-permute-start.11 = (bf16[2,7,24,768]{3,2,1,0:T(8,128)(2,1)S(1)}, bf16[2,7,24,768]{3,2,1,0:T(8,128)(2,1)S(1)}, u32[]{:S(2)}, u32[]{:S(2)}) collective-permute-start(bf16[2,7,24,768]{3,2,1,0:T(8,128)(2,1)S(1)} %constant_dynamic-update-slice_fusion), channel_id=1, source_target_pairs={{0,16},{1,9},{2,18},{3,11},{4,20},{5,13},{6,22},{7,15},{8,24},{9,1... | collective-permute-start | bytes 1548296 | tf_op jit(solution)/shard_map/ppermute | solution.py:563
  27.5 7.7 %collective-permute-start.9 = (bf16[21,24,384]{2,1,0:T(8,128)(2,1)S(1)}, bf16[21,24,384]{2,1,0:T(8,128)(2,1)S(1)}, u32[]{:S(2)}, u32[]{:S(2)}) collective-permute-start(bf16[21,24,384]{2,1,0:T(8,128)(2,1)S(1)} %collective-permute-done.5.refs_2_), channel_id=1, source_target_pairs={{0,4},{1,3},{2,6},{3,1},{4,0},{5,7},{6,2},{7,5},{8,12},{9,11},{10,... | collective-permute-start | bytes 1161224 | tf_op jit(solution)/shard_map/ppermute | solution.py:558
  44.1 18.7 %collective-permute-start.14 = (bf16[4,7,24,768]{3,2,1,0:T(8,128)(2,1)}, bf16[4,7,24,768]{3,2,1,0:T(8,128)(2,1)}, u32[]{:S(2)}, u32[]{:S(2)}) collective-permute-start(bf16[4,7,24,768]{3,2,1,0:T(8,128)(2,1)} %constant_dynamic-update-slice_fusion.2.refs_1_), channel_id=1, source_target_pairs={{0,4},{1,3},{2,6},{3,1},{4,0},{5,7},{6,2},{7,5},{8,12},{9,11},{10,... | collective-permute-start | bytes 3096584 | tf_op jit(solution)/shard_map/ppermute | solution.py:558
  45.6 17.2 %collective-permute-start.13 = (bf16[4,7,24,768]{3,2,1,0:T(8,128)(2,1)}, bf16[4,7,24,768]{3,2,1,0:T(8,128)(2,1)}, u32[]{:S(2)}, u32[]{:S(2)}) collective-permute-start(bf16[4,7,24,768]{3,2,1,0:T(8,128)(2,1)} %constant_dynamic-update-slice_fusion.2.refs_1_), channel_id=1, source_target_pairs={{0,2},{1,5},{2,0},{3,7},{4,6},{5,1},{6,4},{7,3},{8,10},{9,13},{10,... | collective-permute-start | bytes 3096584 | tf_op jit(solution)/shard_map/ppermute | solution.py:558
  46.7 2.3 collective-permute-start.17
  47.9 12.6 %collective-permute-start.12 = (bf16[1,4,2,24,768]{4,3,2,1,0:T(8,128)(2,1)S(1)}, bf16[1,4,2,24,768]{4,3,2,1,0:T(8,128)(2,1)}, u32[]{:S(2)}, u32[]{:S(2)}) collective-permute-start(bf16[1,4,2,24,768]{4,3,2,1,0:T(8,128)(2,1)S(1)} %maximum_bitcast_fusion), channel_id=1, source_target_pairs={{0,8},{1,17},{2,10},{3,19},{4,12},{5,21},{6,14},{7,23},{8,0},{9,25... | collective-permute-start | bytes 884744 | tf_op jit(solution)/shard_map/ppermute | solution.py:563
  62.8 20.5 %collective-permute-start.19 = (bf16[4,7,24,768]{3,2,1,0:T(8,128)(2,1)}, bf16[4,7,24,768]{3,2,1,0:T(8,128)(2,1)S(1)}, u32[]{:S(2)}, u32[]{:S(2)}) collective-permute-start(bf16[4,7,24,768]{3,2,1,0:T(8,128)(2,1)} %constant_dynamic-update-slice_fusion.2.refs_1_), channel_id=1, source_target_pairs={{0,1},{1,0},{2,3},{3,2},{4,5},{5,4},{6,7},{7,6},{8,9},{9,8},{10,11... | collective-permute-start | bytes 3096584 | tf_op jit(solution)/shard_map/ppermute | solution.py:571
  62.8 20.6 %collective-permute-start.21 = (bf16[4,7,24,768]{3,2,1,0:T(8,128)(2,1)}, bf16[4,7,24,768]{3,2,1,0:T(8,128)(2,1)S(1)}, u32[]{:S(2)}, u32[]{:S(2)}) collective-permute-start(bf16[4,7,24,768]{3,2,1,0:T(8,128)(2,1)} %collective-permute-done.14.refs_3_), channel_id=1, source_target_pairs={{0,1},{1,0},{2,3},{3,2},{4,5},{5,4},{6,7},{7,6},{8,9},{9,8},{10,11... | collective-permute-start | bytes 3096584 | tf_op jit(solution)/shard_map/ppermute | solution.py:571
  63.3 20.1 %collective-permute-start.20 = (bf16[4,7,24,768]{3,2,1,0:T(8,128)(2,1)}, bf16[4,7,24,768]{3,2,1,0:T(8,128)(2,1)S(1)}, u32[]{:S(2)}, u32[]{:S(2)}) collective-permute-start(bf16[4,7,24,768]{3,2,1,0:T(8,128)(2,1)} %collective-permute-done.13.refs_2_), channel_id=1, source_target_pairs={{0,1},{1,0},{2,3},{3,2},{4,5},{5,4},{6,7},{7,6},{8,9},{9,8},{10,11... | collective-permute-start | bytes 3096584 | tf_op jit(solution)/shard_map/ppermute | solution.py:571
  63.3 20.1 %collective-permute-start.18 = (bf16[4,7,24,768]{3,2,1,0:T(8,128)(2,1)}, bf16[4,7,24,768]{3,2,1,0:T(8,128)(2,1)}, u32[]{:S(2)}, u32[]{:S(2)}) collective-permute-start(bf16[4,7,24,768]{3,2,1,0:T(8,128)(2,1)} %collective-permute-done.13.refs_2_), channel_id=1, source_target_pairs={{0,4},{1,3},{2,6},{3,1},{4,0},{5,7},{6,2},{7,5},{8,12},{9,11},{10,... | collective-permute-start | bytes 3096584 | tf_op jit(solution)/shard_map/ppermute | solution.py:558
  66.1 17.3 %collective-permute-start.22 = (bf16[2,4,2,24,768]{4,3,2,1,0:T(8,128)(2,1)S(1)}, bf16[2,4,2,24,768]{4,3,2,1,0:T(8,128)(2,1)}, u32[]{:S(2)}, u32[]{:S(2)}) collective-permute-start(bf16[2,4,2,24,768]{4,3,2,1,0:T(8,128)(2,1)S(1)} %constant_dynamic-update-slice_fusion.4.refs_9_), channel_id=1, source_target_pairs={{0,16},{1,9},{2,18},{3,11},{4,20},{5,13},{6,22},{7,15},{8,24},{9,1... | collective-permute-start | bytes 1769480 | tf_op jit(solution)/shard_map/ppermute | solution.py:563
  83.4 5.7 %collective-permute-start.23 = (bf16[4,7,24,768]{3,2,1,0:T(8,128)(2,1)}, bf16[4,7,24,768]{3,2,1,0:T(8,128)(2,1)}, u32[]{:S(2)}, u32[]{:S(2)}) collective-permute-start(bf16[4,7,24,768]{3,2,1,0:T(8,128)(2,1)} %collective-permute-done.18.refs_4_), channel_id=1, source_target_pairs={{0,1},{1,0},{2,3},{3,2},{4,5},{5,4},{6,7},{7,6},{8,9},{9,8},{10,11... | collective-permute-start | bytes 3096584 | tf_op jit(solution)/shard_map/ppermute | solution.py:571
  83.5 3.9 %collective-permute-start.24 = (bf16[2,4,2,24,768]{4,3,2,1,0:T(8,128)(2,1)S(1)}, bf16[2,4,2,24,768]{4,3,2,1,0:T(8,128)(2,1)S(1)}, u32[]{:S(2)}, u32[]{:S(2)}) collective-permute-start(bf16[2,4,2,24,768]{4,3,2,1,0:T(8,128)(2,1)S(1)} %constant_dynamic-update-slice_fusion.4.refs_9_), channel_id=1, source_target_pairs={{0,1},{1,0},{2,3},{3,2},{4,5},{5,4},{6,7},{7,6},{8,9},{9,8},{10,11... | collective-permute-start | bytes 1769480 | tf_op jit(solution)/shard_map/ppermute | solution.py:571
  84.0 4.3 %collective-permute-start.25 = (bf16[2,4,2,24,768]{4,3,2,1,0:T(8,128)(2,1)}, bf16[2,4,2,24,768]{4,3,2,1,0:T(8,128)(2,1)S(1)}, u32[]{:S(2)}, u32[]{:S(2)}) collective-permute-start(bf16[2,4,2,24,768]{4,3,2,1,0:T(8,128)(2,1)} %collective-permute-done.22.refs_10_), channel_id=1, source_target_pairs={{0,1},{1,0},{2,3},{3,2},{4,5},{5,4},{6,7},{7,6},{8,9},{9,8},{10,11... | collective-permute-start | bytes 1769480 | tf_op jit(solution)/shard_map/ppermute | solution.py:571
  136.0 11.0 %collective-permute-start.26 = (bf16[8,5,24,768]{3,2,1,0:T(8,128)(2,1)}, bf16[8,5,24,768]{3,2,1,0:T(8,128)(2,1)S(1)}, u32[]{:S(2)}, u32[]{:S(2)}) collective-permute-start(bf16[8,5,24,768]{3,2,1,0:T(8,128)(2,1)} %bitcast.42), channel_id=1, source_target_pairs={{0,1},{1,0},{2,3},{3,2},{4,5},{5,4},{6,7},{7,6},{8,9},{9,8},{10,11... | collective-permute-start | bytes 4423688 | tf_op jit(solution)/shard_map/ppermute | solution.py:571
  136.4 10.6 %collective-permute-start.27 = (bf16[8,5,24,768]{3,2,1,0:T(8,128)(2,1)}, bf16[8,5,24,768]{3,2,1,0:T(8,128)(2,1)}, u32[]{:S(2)}, u32[]{:S(2)}) collective-permute-start(bf16[8,5,24,768]{3,2,1,0:T(8,128)(2,1)} %bitcast.41), channel_id=1, source_target_pairs={{0,1},{1,0},{2,3},{3,2},{4,5},{5,4},{6,7},{7,6},{8,9},{9,8},{10,11... | collective-permute-start | bytes 4423688 | tf_op jit(solution)/shard_map/ppermute | solution.py:571
  146.6 5.1 %collective-permute-start.28 = (bf16[8,4,24,768]{3,2,1,0:T(8,128)(2,1)}, bf16[8,4,24,768]{3,2,1,0:T(8,128)(2,1)S(1)}, u32[]{:S(2)}, u32[]{:S(2)}) collective-permute-start(bf16[8,4,24,768]{3,2,1,0:T(8,128)(2,1)} %get-tuple-element.177), channel_id=1, source_target_pairs={{0,1},{1,0},{2,3},{3,2},{4,5},{5,4},{6,7},{7,6},{8,9},{9,8},{10,11... | collective-permute-start | bytes 3538952 | tf_op jit(solution)/shard_map/ppermute | solution.py:571
  150.0 37.0 %collective-permute-start.31 = (bf16[8,5,24,768]{3,2,1,0:T(8,128)(2,1)}, bf16[8,5,24,768]{3,2,1,0:T(8,128)(2,1)S(1)}, u32[]{:S(2)}, u32[]{:S(2)}) collective-permute-start(bf16[8,5,24,768]{3,2,1,0:T(8,128)(2,1)} %fusion.refs_8_), channel_id=1, source_target_pairs={{0,2},{1,5},{2,0},{3,7},{4,6},{5,1},{6,4},{7,3},{8,10},{9,13},{10,... | collective-permute-start | bytes 4423688 | tf_op jit(solution)/shard_map/ppermute | solution.py:558
  153.0 33.9 %collective-permute-start.32 = (bf16[8,4,24,768]{3,2,1,0:T(8,128)(2,1)}, bf16[8,4,24,768]{3,2,1,0:T(8,128)(2,1)}, u32[]{:S(2)}, u32[]{:S(2)}) collective-permute-start(bf16[8,4,24,768]{3,2,1,0:T(8,128)(2,1)} %add_convert_fusion.refs_9_), channel_id=1, source_target_pairs={{0,8},{1,17},{2,10},{3,19},{4,12},{5,21},{6,14},{7,23},{8,0},{9,25... | collective-permute-start | bytes 3538952 | tf_op jit(solution)/shard_map/ppermute | solution.py:563
  153.1 33.9 %collective-permute-start.33 = (bf16[8,4,24,768]{3,2,1,0:T(8,128)(2,1)}, bf16[8,4,24,768]{3,2,1,0:T(8,128)(2,1)}, u32[]{:S(2)}, u32[]{:S(2)}) collective-permute-start(bf16[8,4,24,768]{3,2,1,0:T(8,128)(2,1)} %get-tuple-element.197), channel_id=1, source_target_pairs={{0,1},{1,0},{2,3},{3,2},{4,5},{5,4},{6,7},{7,6},{8,9},{9,8},{10,11... | collective-permute-start | bytes 3538952 | tf_op jit(solution)/shard_map/ppermute | solution.py:571
  186.3 2.6 %collective-permute-start.29 = (bf16[8,5,24,384]{3,2,1,0:T(8,128)(2,1)}, bf16[8,5,24,384]{3,2,1,0:T(8,128)(2,1)S(1)}, u32[]{:S(2)}, u32[]{:S(2)}) collective-permute-start(bf16[8,5,24,384]{3,2,1,0:T(8,128)(2,1)} %get-tuple-element.191), channel_id=1, source_target_pairs={{0,1},{1,0},{2,3},{3,2},{4,5},{5,4},{6,7},{7,6},{8,9},{9,8},{10,11... | collective-permute-start | bytes 2211848 | tf_op jit(solution)/shard_map/ppermute | solution.py:571
  186.9 3.1 %collective-permute-start.30 = (bf16[8,5,24,384]{3,2,1,0:T(8,128)(2,1)}, bf16[8,5,24,384]{3,2,1,0:T(8,128)(2,1)S(1)}, u32[]{:S(2)}, u32[]{:S(2)}) collective-permute-start(bf16[8,5,24,384]{3,2,1,0:T(8,128)(2,1)} %get-tuple-element.192), channel_id=1, source_target_pairs={{0,1},{1,0},{2,3},{3,2},{4,5},{5,4},{6,7},{7,6},{8,9},{9,8},{10,11... | collective-permute-start | bytes 2211848 | tf_op jit(solution)/shard_map/ppermute | solution.py:571
  190.2 19.0 %collective-permute-start.34 = (bf16[8,5,24,384]{3,2,1,0:T(8,128)(2,1)S(1)}, bf16[8,5,24,384]{3,2,1,0:T(8,128)(2,1)S(1)}, u32[]{:S(2)}, u32[]{:S(2)}) collective-permute-start(bf16[8,5,24,384]{3,2,1,0:T(8,128)(2,1)S(1)} %add_convert_fusion.1.refs_14_), channel_id=1, source_target_pairs={{0,2},{1,5},{2,0},{3,7},{4,6},{5,1},{6,4},{7,3},{8,10},{9,13},{10,... | collective-permute-start | bytes 2211848 | tf_op jit(solution)/shard_map/ppermute | solution.py:558
  190.7 18.5 %collective-permute-start.35 = (bf16[4,5,24,768]{3,2,1,0:T(8,128)(2,1)S(1)}, bf16[4,5,24,768]{3,2,1,0:T(8,128)(2,1)S(1)}, u32[]{:S(2)}, u32[]{:S(2)}) collective-permute-start(bf16[4,5,24,768]{3,2,1,0:T(8,128)(2,1)S(1)} %fusion.2.refs_15_), channel_id=1, source_target_pairs={{0,4},{1,3},{2,6},{3,1},{4,0},{5,7},{6,2},{7,5},{8,12},{9,11},{10,... | collective-permute-start | bytes 2211848 | tf_op jit(solution)/shard_map/ppermute | solution.py:558
  192.0 17.1 %collective-permute-start.36 = (bf16[4,4,24,768]{3,2,1,0:T(8,128)(2,1)S(1)}, bf16[4,4,24,768]{3,2,1,0:T(8,128)(2,1)S(1)}, u32[]{:S(2)}, u32[]{:S(2)}) collective-permute-start(bf16[4,4,24,768]{3,2,1,0:T(8,128)(2,1)S(1)} %add_convert_fusion.2.refs_16_), channel_id=1, source_target_pairs={{0,16},{1,9},{2,18},{3,11},{4,20},{5,13},{6,22},{7,15},{8,24},{9,1... | collective-permute-start | bytes 1769480 | tf_op jit(solution)/shard_map/ppermute | solution.py:563
  209.3 14.7 %collective-permute-start.37 = (bf16[4,5,24,384]{3,2,1,0:T(8,128)(2,1)S(1)}, bf16[4,5,24,384]{3,2,1,0:T(8,128)(2,1)S(1)}, u32[]{:S(2)}, u32[]{:S(2)}) collective-permute-start(bf16[4,5,24,384]{3,2,1,0:T(8,128)(2,1)S(1)} %add_convert_fusion.4.refs_5_), channel_id=1, source_target_pairs={{0,4},{1,3},{2,6},{3,1},{4,0},{5,7},{6,2},{7,5},{8,12},{9,11},{10,... | collective-permute-start | bytes 1105928 | tf_op jit(solution)/shard_map/ppermute | solution.py:558
  210.3 13.7 %collective-permute-start.38 = (bf16[2,5,24,768]{3,2,1,0:T(8,128)(2,1)S(1)}, bf16[2,5,24,768]{3,2,1,0:T(8,128)(2,1)S(1)}, u32[]{:S(2)}, u32[]{:S(2)}) collective-permute-start(bf16[2,5,24,768]{3,2,1,0:T(8,128)(2,1)S(1)} %add_convert_fusion.3.refs_6_), channel_id=1, source_target_pairs={{0,8},{1,17},{2,10},{3,19},{4,12},{5,21},{6,14},{7,23},{8,0},{9,25... | collective-permute-start | bytes 1105928 | tf_op jit(solution)/shard_map/ppermute | solution.py:563
  213.1 11.0 %collective-permute-start.39 = (bf16[2,4,24,768]{3,2,1,0:T(8,128)(2,1)S(1)}, bf16[2,4,24,768]{3,2,1,0:T(8,128)(2,1)S(1)}, u32[]{:S(2)}, u32[]{:S(2)}) collective-permute-start(bf16[2,4,24,768]{3,2,1,0:T(8,128)(2,1)S(1)} %add_convert_fusion.5.refs_7_), channel_id=1, source_target_pairs={{0,2},{1,5},{2,0},{3,7},{4,6},{5,1},{6,4},{7,3},{8,10},{9,13},{10,... | collective-permute-start | bytes 884744 | tf_op jit(solution)/shard_map/ppermute | solution.py:558
  214.7 9.3 %collective-permute-start.40 = (f32[4,1104]{1,0:T(4,128)S(1)}, f32[4,1104]{1,0:T(4,128)S(1)}, u32[]{:S(2)}, u32[]{:S(2)}) collective-permute-start(f32[4,1104]{1,0:T(4,128)S(1)} %get-tuple-element.212), channel_id=1, source_target_pairs={{0,1},{1,0},{2,3},{3,2},{4,5},{5,4},{6,7},{7,6},{8,9},{9,8},{10,11... | collective-permute-start | bytes 53000 | tf_op jit(solution)/shard_map/ppermute | solution.py:571
  224.2 7.1 %collective-permute-start.44 = (bf16[2,5,24,384]{3,2,1,0:T(8,128)(2,1)S(1)}, bf16[2,5,24,384]{3,2,1,0:T(8,128)(2,1)S(1)}, u32[]{:S(2)}, u32[]{:S(2)}) collective-permute-start(bf16[2,5,24,384]{3,2,1,0:T(8,128)(2,1)S(1)} %add_convert_fusion.7), channel_id=1, source_target_pairs={{0,8},{1,17},{2,10},{3,19},{4,12},{5,21},{6,14},{7,23},{8,0},{9,25... | collective-permute-start | bytes 552968 | tf_op jit(solution)/shard_map/ppermute | solution.py:563
  225.0 7.4 %collective-permute-start.43 = (f32[1104]{0:T(1024)S(1)}, f32[1104]{0:T(1024)S(1)}, u32[]{:S(2)}, u32[]{:S(2)}) collective-permute-start(f32[1104]{0:T(1024)S(1)} %get-tuple-element.232), channel_id=1, source_target_pairs={{0,6},{1,7},{2,4},{3,5},{4,2},{5,3},{6,0},{7,1},{8,14},{9,15},{10,... | collective-permute-start | bytes 13256 | tf_op jit(solution)/shard_map/ppermute | solution.py:571
  226.2 6.2 %collective-permute-start.42 = (f32[1104]{0:T(1024)S(1)}, f32[1104]{0:T(1024)S(1)}, u32[]{:S(2)}, u32[]{:S(2)}) collective-permute-start(f32[1104]{0:T(1024)S(1)} %get-tuple-element.233), channel_id=1, source_target_pairs={{0,4},{1,5},{2,6},{3,7},{4,0},{5,1},{6,2},{7,3},{8,12},{9,13},{10,... | collective-permute-start | bytes 13256 | tf_op jit(solution)/shard_map/ppermute | solution.py:571
  226.9 5.5 %collective-permute-start.41 = (f32[1104]{0:T(1024)S(1)}, f32[1104]{0:T(1024)S(1)}, u32[]{:S(2)}, u32[]{:S(2)}) collective-permute-start(f32[1104]{0:T(1024)S(1)} %get-tuple-element.234), channel_id=1, source_target_pairs={{0,2},{1,3},{2,0},{3,1},{4,6},{5,7},{6,4},{7,5},{8,10},{9,11},{10,... | collective-permute-start | bytes 13256 | tf_op jit(solution)/shard_map/ppermute | solution.py:571
  229.6 7.3 %collective-permute-start.50 = (bf16[1,4,24,768]{3,2,1,0:T(8,128)(2,1)S(1)}, bf16[1,4,24,768]{3,2,1,0:T(8,128)(2,1)S(1)}, u32[]{:S(2)}, u32[]{:S(2)}) collective-permute-start(bf16[1,4,24,768]{3,2,1,0:T(8,128)(2,1)S(1)} %add_convert_fusion.8), channel_id=1, source_target_pairs={{0,4},{1,3},{2,6},{3,1},{4,0},{5,7},{6,2},{7,5},{8,12},{9,11},{10,... | collective-permute-start | bytes 442376 | tf_op jit(solution)/shard_map/ppermute | solution.py:558
  231.2 9.0 %collective-permute-start.49 = (bf16[1,5,24,768]{3,2,1,0:T(8,128)(2,1)S(1)}, bf16[1,5,24,768]{3,2,1,0:T(8,128)(2,1)S(1)}, u32[]{:S(2)}, u32[]{:S(2)}) collective-permute-start(bf16[1,5,24,768]{3,2,1,0:T(8,128)(2,1)S(1)} %add_convert_fusion.6), channel_id=1, source_target_pairs={{0,16},{1,9},{2,18},{3,11},{4,20},{5,13},{6,22},{7,15},{8,24},{9,1... | collective-permute-start | bytes 552968 | tf_op jit(solution)/shard_map/ppermute | solution.py:563
  232.4 9.7 %collective-permute-start.47 = (f32[1104]{0:T(1024)S(1)}, f32[1104]{0:T(1024)S(1)}, u32[]{:S(2)}, u32[]{:S(2)}) collective-permute-start(f32[1104]{0:T(1024)S(1)} %add_add_fusion.1), channel_id=1, source_target_pairs={{0,24},{8,16},{16,8},{24,0},{1,25},{9,17},{17,9},{25,1},{2,26},{10... | collective-permute-start | bytes 13256 | tf_op jit(solution)/shard_map/ppermute | solution.py:567
  234.7 7.4 %collective-permute-start.46 = (f32[1104]{0:T(1024)S(1)}, f32[1104]{0:T(1024)S(1)}, u32[]{:S(2)}, u32[]{:S(2)}) collective-permute-start(f32[1104]{0:T(1024)S(1)} %add_add_fusion.1), channel_id=1, source_target_pairs={{0,16},{8,24},{16,0},{24,8},{1,17},{9,25},{17,1},{25,9},{2,18},{10... | collective-permute-start | bytes 13256 | tf_op jit(solution)/shard_map/ppermute | solution.py:567
  235.0 7.1 %collective-permute-start.45 = (f32[1104]{0:T(1024)S(1)}, f32[1104]{0:T(1024)S(1)}, u32[]{:S(2)}, u32[]{:S(2)}) collective-permute-start(f32[1104]{0:T(1024)S(1)} %add_add_fusion.1), channel_id=1, source_target_pairs={{0,8},{8,0},{16,24},{24,16},{1,9},{9,1},{17,25},{25,17},{2,10},{10... | collective-permute-start | bytes 13256 | tf_op jit(solution)/shard_map/ppermute | solution.py:567
  236.9 6.0 %collective-permute-start.48 = (bf16[1,5,24,384]{3,2,1,0:T(8,128)(2,1)S(1)}, bf16[1,5,24,384]{3,2,1,0:T(8,128)(2,1)S(1)}, u32[]{:S(2)}, u32[]{:S(2)}) collective-permute-start(bf16[1,5,24,384]{3,2,1,0:T(8,128)(2,1)S(1)} %add_convert_fusion.9), channel_id=1, source_target_pairs={{0,16},{1,9},{2,18},{3,11},{4,20},{5,13},{6,22},{7,15},{8,24},{9,1... | collective-permute-start | bytes 276488 | tf_op jit(solution)/shard_map/ppermute | solution.py:563
  (39 other events, 277.6 us)
